TPU v7x, 32 devices: a whole 2x2x4 slice. The times are simulated.
32 devices in a mesh: grp: 4 (over y, x), blk: 8 (over z, core).
Axes of the slice: x: 2, y: 2, z: 4, core: 2. Of those that a mesh axis runs over, the one named last changes fastest.
Arguments:
- queries: bfloat16 [4096, 4096], P(('grp', 'blk')), may hold values from -4 to 4
- passages: bfloat16 [4096, 4096], P(('grp', 'blk')), may hold values from -1 to 1
- hard_index: int32 [4096, 3], P(('grp', 'blk')), may hold values from 0 to 4095, as said below
- weights: float32 [4096], P(('grp', 'blk')), may hold values from 0.5 to 2
Outputs:
- loss_rows: float32 [4096], P(('grp', 'blk'))
- grad_queries: bfloat16 [4096, 4096], P(('grp', 'blk'))
- grad_passages: bfloat16 [4096, 4096], P(('grp', 'blk'))
Inputs may be any that keep to these rules, and one draw needn't show every extreme that they name: `hard_index`: the three entries of query i name passages of the block at the same index of blk as query i in three different groups, none its own; among the queries of one device at most 128 entries name one group, and in every device exactly 128 entries name some group.
All inputs are finite; a program needn't handle non-finite values.
Results may differ from a plain program's by a relative error of at most 0.0065.
Values may be sent and summed in bfloat16 or wider, within the bound.
No kernel may reach another device: no remote copies, remote signals or barrier semaphores. Data moves between devices by JAX's collectives and lax.ppermute only.
A program may use at most 64 MiB of HBM per device.

v0:
```python
import functools
import math

import jax
import jax.numpy as jnp
from jax import lax
from jax.experimental import pallas as pl
from jax.experimental.pallas import tpu as pltpu
from jax.sharding import PartitionSpec as P

INV_TEMP = 50.0
BF16 = jnp.bfloat16
F32 = jnp.float32
CHUNK = 512
TAIL = 16
LONG, SOME = 5 * 10**10, 16 * 10**9
VMEM = pl.BlockSpec(memory_space=pltpu.VMEM)
HBM = pl.BlockSpec(memory_space=pltpu.HBM)
TOKEN = jax.ShapeDtypeStruct((8, 128), F32)


def dot(left, right, dims):
    return lax.dot_general(left, right, (dims, ((), ())), preferred_element_type=F32)


def size_of(arrays):
    return sum(math.prod(a.shape) * jnp.dtype(a.dtype).itemsize for a in arrays)


def local_call(body, out_shape, *args, flops=0, in_specs=None, out_specs=None, scratch=()):
    return pl.pallas_call(
        body,
        out_shape=out_shape,
        in_specs=in_specs or [VMEM] * len(args),
        out_specs=out_specs or [VMEM] * len(out_shape),
        scratch_shapes=list(scratch),
        cost_estimate=pl.CostEstimate(
            flops=flops, bytes_accessed=size_of(args) + size_of(out_shape), transcendentals=0
        ),
        compiler_params=pltpu.CompilerParams(vmem_limit_bytes=20 * 2**20),
    )(*args)


def signal(token):
    token[...] = jnp.zeros(token.shape, token.dtype)


def split_index(index, rows, group_rows):
    if group_rows & (group_rows - 1) or rows & (rows - 1):
        return index // group_rows, index % rows
    return index >> (group_rows.bit_length() - 1), index & (rows - 1)


def load_body(groups, group_rows, q_hbm, p_hbm, index_ref, q_ref, p_ref, *refs):
    pieces, token, sems = refs[:groups], refs[groups], refs[groups + 1]
    rows = q_ref.shape[0]
    cols = pieces[0].shape[1]
    g = lax.axis_index("grp")
    copies = []
    for r in range(groups):
        at = pl.ds(pl.multiple_of((g ^ r) * cols, 128), cols)
        pair = [
            pltpu.make_async_copy(source.at[:, at], target.at[:, at], sems.at[2 * r + n])
            for n, (source, target) in enumerate(((q_hbm, q_ref), (p_hbm, p_ref)))
        ]
        for copy in pair:
            copy.start()
        copies.append((at, pair))
    signal(token)
    index = jnp.concatenate([index_ref[...], jnp.zeros((TAIL - 3, rows), jnp.int32)], axis=0)
    named_group, named_row = split_index(index, rows, group_rows)
    named_group = named_group.astype(F32).astype(BF16)
    named_row = named_row.astype(F32).astype(BF16)
    for r in reversed(range(groups)):
        at, pair = copies[r]
        for copy in pair:
            copy.wait()
        pieces[r][:rows] = q_ref[:, at]
        pieces[r][rows : 2 * rows] = p_ref[:, at]
        pieces[r][2 * rows :, :rows] = named_group
        pieces[r][2 * rows :, rows : 2 * rows] = named_row


def places_of(piece_ref, rows):
    tail = piece_ref[2 * rows :, : 2 * rows].astype(F32).astype(jnp.int32)
    g = lax.axis_index("grp")
    return [(tail[k : k + 1, :rows] ^ g) * rows + tail[k : k + 1, rows:] for k in range(3)]


def hard_scores_body(groups, *refs):
    pieces, outs = refs[:groups], refs[groups + 1 :]
    rows = outs[0].shape[1]
    ids = lax.broadcasted_iota(jnp.int32, (groups * rows, rows), 0)
    p_all = jnp.concatenate([piece[rows : 2 * rows] for piece in pieces], axis=0)
    for r in range(groups):
        places = places_of(pieces[r], rows)
        dots = dot(p_all, pieces[r][:rows], ((1,), (1,)))
        for k in range(3):
            hit = jnp.where(ids == places[k], dots, 0.0)
            outs[r][k : k + 1] = jnp.sum(hit, axis=0, keepdims=True)


def hard_grads_body(groups, *refs):
    pieces, coefs, outs = refs[:groups], refs[groups : 2 * groups], refs[2 * groups + 1 : 3 * groups + 1]
    token, matrix, matrix_t = refs[3 * groups + 1 :]
    rows = coefs[0].shape[1]
    cols = outs[0].shape[1]
    signal(token)
    ids = lax.broadcasted_iota(jnp.int32, (groups * rows, rows), 0)
    for r in range(groups):
        places = places_of(pieces[r], rows)
        total = jnp.zeros(ids.shape, F32)
        for k in range(3):
            total += jnp.where(ids == places[k], coefs[r][k : k + 1], 0.0)
        mine = slice(r * rows, (r + 1) * rows)
        matrix[:, mine] = total.astype(BF16)
        matrix_t[mine] = total.T.astype(BF16)
    step = min(cols, 256)
    for c in range(0, cols, step):
        at = slice(c, c + step)
        q_all = jnp.concatenate([piece[:rows, at] for piece in pieces], axis=0)
        p_all = jnp.concatenate([piece[rows : 2 * rows, at] for piece in pieces], axis=0)
        grad_q = dot(matrix_t[...], p_all, ((1,), (0,))).astype(BF16)
        grad_p = dot(matrix[...], q_all, ((1,), (0,))).astype(BF16)
        for r in range(groups):
            mine = slice(r * rows, (r + 1) * rows)
            outs[r][:rows, at] = grad_q[mine]
            outs[r][rows:, at] = grad_p[mine]


def pass_body(source, token, out):
    out[...] = source[...]


def choose_body(n1_ref, e3_ref, out):
    odd = lax.axis_index("blk") % 2 == 1

    @pl.when(odd)
    def _():
        out[...] = n1_ref[...]

    @pl.when(jnp.logical_not(odd))
    def _():
        out[...] = e3_ref[...]


def scores_body(q_ref, *refs):
    half = len(refs) // 2
    for block, out in zip(refs[:half], refs[half:]):
        out[...] = dot(block[...], q_ref[...], ((1,), (1,)))


def weigh_body(groups, q_ref, s0_ref, s1_ref, s2_ref, s3_ref, last_ref, w_ref, *refs):
    hard_refs = refs[:groups]
    loss_ref, coef_ref, hard_out, term3_ref, term2_ref = refs[groups:]
    rows, width = q_ref.shape
    w = w_ref[...]
    s3 = INV_TEMP * (s3_ref[...] + dot(last_ref[...], q_ref[...], ((1,), (1,))))
    scores = [INV_TEMP * s0_ref[...], INV_TEMP * s1_ref[...], INV_TEMP * s2_ref[...], s3]
    hard = hard_refs[0][...]
    for other in hard_refs[1:]:
        hard = hard + other[...]
    hard = INV_TEMP * hard
    largest = jnp.max(hard, axis=0, keepdims=True)
    for block in scores:
        largest = jnp.maximum(largest, jnp.max(block, axis=0, keepdims=True))
    summed = jnp.sum(jnp.exp(hard - largest), axis=0, keepdims=True)
    for block in scores:
        summed = summed + jnp.sum(jnp.exp(block - largest), axis=0, keepdims=True)
    log_total = largest + jnp.log(summed)
    for s in range(4):
        coef_ref[s * rows : (s + 1) * rows] = (w * jnp.exp(scores[s] - log_total)).astype(BF16)
    for c in range(0, width, CHUNK):
        at = slice(c, c + CHUNK)
        both = dot(coef_ref[2 * rows :], q_ref[:, at], ((1,), (0,))).astype(BF16)
        term2_ref[:, at] = both[:rows]
        term3_ref[:, at] = both[rows:]
    hard_out[...] = (w * jnp.exp(hard - log_total)).astype(BF16).astype(F32)
    eye = lax.broadcasted_iota(jnp.int32, (rows, rows), 0) == lax.broadcasted_iota(
        jnp.int32, (rows, rows), 1
    )
    loss_ref[...] = log_total - jnp.sum(jnp.where(eye, scores[0], 0.0), axis=0, keepdims=True)


def add_body(a_ref, b_ref, out, token):
    signal(token)
    out[...] = (a_ref[...].astype(F32) + b_ref[...].astype(F32)).astype(BF16)


def term1_body(q_ref, coef_ref, got2_ref, token, out):
    rows, width = q_ref.shape
    keep = jnp.where(lax.axis_index("blk") % 2 == 1, 1.0, 0.0)
    for c in range(0, width, CHUNK):
        at = slice(c, c + CHUNK)
        term1 = dot(coef_ref[rows : 2 * rows], q_ref[:, at], ((1,), (0,)))
        out[:, at] = term1 + keep * got2_ref[:, at].astype(F32)


def relay_body(partial1, got3_ref, out, done):
    signal(done)
    out[...] = (partial1[...] + got3_ref[...].astype(F32)).astype(BF16)


def base_body(
    q_ref, p_ref, n1_ref, n2_ref, e3_ref, o3_ref, coef_ref, w_ref, own3_ref, token, pulled, base
):
    rows, width = q_ref.shape
    w = jnp.broadcast_to(w_ref[...], (rows, rows)).T[:, :1]
    blocks = (p_ref, n1_ref, n2_ref, e3_ref, o3_ref)
    coef_t = coef_ref[...].astype(F32).T.astype(BF16)
    coef_t = jnp.concatenate([coef_t, coef_t[:, 3 * rows :]], axis=1)
    for c in range(0, width, CHUNK):
        at = slice(c, c + CHUNK)
        held = jnp.concatenate([block[:, at] for block in blocks], axis=0)
        pulled[:, at] = dot(coef_t, held, ((1,), (0,))) - w * p_ref[:, at].astype(F32)
        own = dot(coef_ref[:rows], q_ref[:, at], ((1,), (0,))) + own3_ref[:, at].astype(F32)
        base[:, at] = own - w * q_ref[:, at].astype(F32)


def finish_body(groups, pulled, base, own1, *refs):
    backs = refs[:groups]
    q_out, p_out, q_held, p_held, sems = refs[groups:]
    rows, cols = pulled.shape[0], backs[0].shape[1]
    g = lax.axis_index("grp")
    copies = []
    for r, back in enumerate(backs):
        at = pl.ds(pl.multiple_of((g ^ r) * cols, 128), cols)
        q_held[:, at] = (INV_TEMP * (pulled[:, at] + back[:rows].astype(F32))).astype(BF16)
        copies.append(pltpu.make_async_copy(q_held.at[:, at], q_out.at[:, at], sems.at[2 * r]))
        copies[-1].start()
        total = base[:, at] + back[rows:].astype(F32) + own1[:, at].astype(F32)
        p_held[:, at] = (INV_TEMP * total).astype(BF16)
        copies.append(pltpu.make_async_copy(p_held.at[:, at], p_out.at[:, at], sems.at[2 * r + 1]))
        copies[-1].start()
    for copy in copies:
        copy.wait()


def per_device(queries, passages, hard_index, weights):
    rows, width = queries.shape
    groups = lax.axis_size("grp")
    loop = lax.axis_size("blk")
    cols = width // groups

    def shift(array, by, which=(0, 1)):
        pairs = [(i, (i + by) % loop) for i in range(loop) if i % 2 in which]
        return lax.ppermute(array, "blk", pairs)

    def swap(array):
        return lax.ppermute(array, "blk", [(i, i ^ 1) for i in range(loop)])

    def exchange(arrays):
        out = list(arrays)
        for r in reversed(range(1, groups)):
            out[r] = lax.ppermute(arrays[r], "grp", [(i, i ^ r) for i in range(groups)])
        return out

    def like(*shape, dtype=BF16):
        return jax.ShapeDtypeStruct(shape, dtype)

    block, block32 = like(rows, width), like(rows, width, dtype=F32)
    square, triple = like(rows, rows, dtype=F32), like(3, rows, dtype=F32)
    piece, back = like(2 * rows + TAIL, cols), like(2 * rows, cols)

    next1 = shift(passages, -1)

    held_q, held_p, *pieces, token = local_call(
        functools.partial(load_body, groups, loop * rows),
        [block, block] + [piece] * groups + [TOKEN],
        queries, passages, hard_index.T,
        in_specs=[HBM, HBM, VMEM],
        scratch=[pltpu.SemaphoreType.DMA((2 * groups,))],
    )
    pieces = exchange(pieces)

    next3_even = shift(held_p, -3, (1,))
    (next1,) = local_call(pass_body, [block], next1, token, flops=LONG)
    next3_odd = shift(next1, -2, (1,))
    next2 = swap(local_call(choose_body, [block], next1, next3_even, flops=LONG)[0])

    s0, s1, s3 = local_call(scores_body, [square] * 3, held_q, held_p, next1, next3_even)
    hard_parts = exchange(
        local_call(
            functools.partial(hard_scores_body, groups), [triple] * groups, *pieces, s0, flops=LONG
        )
    )
    (s2,) = local_call(scores_body, [square], held_q, next2)
    loss_rows, coef, hard_coef, term3, term2 = local_call(
        functools.partial(weigh_body, groups),
        [like(1, rows, dtype=F32), like(4 * rows, rows), triple, block, block],
        held_q, s0, s1, s2, s3, next3_odd, weights[None, :], *hard_parts,
    )

    got3 = shift(term3, 2, (1,))
    got2 = swap(term2)

    sent3, token = local_call(add_body, [block, TOKEN], term3, got2)
    own3 = shift(sent3, 3, (0,))

    hard_coefs = exchange([hard_coef] * groups)
    square_all = pltpu.VMEM((groups * rows, groups * rows), BF16)
    *backs, token = local_call(
        functools.partial(hard_grads_body, groups), [back] * groups + [TOKEN],
        *pieces, *hard_coefs, token, scratch=[square_all, square_all],
    )
    backs = exchange(backs)

    (partial1,) = local_call(term1_body, [block32], held_q, coef, got2, token)
    sent1, token = local_call(relay_body, [block, TOKEN], partial1, got3, flops=SOME)
    own1 = shift(sent1, 1)

    pulled, base = local_call(
        base_body, [block32, block32],
        held_q, held_p, next1, next2, next3_even, next3_odd, coef, weights[None, :], own3, token,
        flops=LONG,
    )
    grad_queries, grad_passages = local_call(
        functools.partial(finish_body, groups), [block, block], pulled, base, own1, *backs,
        out_specs=[HBM, HBM],
        scratch=[
            pltpu.VMEM((rows, width), BF16),
            pltpu.VMEM((rows, width), BF16),
            pltpu.SemaphoreType.DMA((2 * groups,)),
        ],
    )
    return loss_rows.reshape(rows), grad_queries, grad_passages


def solution(mesh):
    rows = P(("grp", "blk"))
    matrix = P(("grp", "blk"), None)
    return jax.shard_map(
        per_device,
        mesh=mesh,
        in_specs=(matrix, matrix, matrix, rows),
        out_specs=(rows, matrix, matrix),
        check_vma=False,
    )
```

profile of v0, /device:TPU:0, one launch (start us, length us, event | category | flops | bytes accessed | tf_op | source)
XLA Modules:
  0.0 87.0 jit_solution(1248738663241903332)
XLA Ops:
  0.6 4.5 %collective-permute-start = (bf16[128,4096]{1,0:T(8,128)(2,1)}, bf16[128,4096]{1,0:T(8,128)(2,1)S(1)}, u32[]{:S(2)}, u32[]{:S(2)}) collective-permute-start(bf16[128,4096]{1,0:T(8,128)(2,1)} %p_hbm.1), channel_id=1, source_target_pairs={{0,7},{1,0},{2,1},{3,2},{4,3},{5,4},{6,5},{7,6},{8,15},{9,8},{10,9... | collective-permute-start | bytes 3145736 | tf_op jit(solution)/shard_map/ppermute | solution.py:247
  5.2 1.2 %copy-done = bf16[128,4096]{1,0:T(8,128)(2,1)S(1)} copy-done((bf16[128,4096]{1,0:T(8,128)(2,1)S(1)}, bf16[128,4096]{1,0:T(8,128)(2,1)}, u32[]{:S(2)}) %copy-start) | copy-done | bytes 1048600
  6.4 1.2 %copy-done.1 = bf16[128,4096]{1,0:T(8,128)(2,1)S(1)} copy-done((bf16[128,4096]{1,0:T(8,128)(2,1)S(1)}, bf16[128,4096]{1,0:T(8,128)(2,1)}, u32[]{:S(2)}) %copy-start.1) | copy-done | bytes 1048600
  8.7 1.6 %collective-permute-start.4 = (bf16[272,1024]{1,0:T(8,128)(2,1)S(1)}, bf16[272,1024]{1,0:T(8,128)(2,1)S(1)}, u32[]{:S(2)}, u32[]{:S(2)}) collective-permute-start(bf16[272,1024]{1,0:T(8,128)(2,1)S(1)} %get-tuple-element.42), channel_id=1, source_target_pairs={{0,8},{8,0},{16,24},{24,16},{1,9},{9,1},{17,25},{25,17},{2,10},{10... | collective-permute-start | bytes 1671176 | tf_op jit(solution)/shard_map/ppermute | solution.py:255
  10.2 1.5 %collective-permute-start.5 = (bf16[272,1024]{1,0:T(8,128)(2,1)S(1)}, bf16[272,1024]{1,0:T(8,128)(2,1)S(1)}, u32[]{:S(2)}, u32[]{:S(2)}) collective-permute-start(bf16[272,1024]{1,0:T(8,128)(2,1)S(1)} %get-tuple-element.43), channel_id=1, source_target_pairs={{0,16},{8,24},{16,0},{24,8},{1,17},{9,25},{17,1},{25,9},{2,18},{10... | collective-permute-start | bytes 1671176 | tf_op jit(solution)/shard_map/ppermute | solution.py:255
  12.2 1.3 %collective-permute-start.1 = (bf16[128,4096]{1,0:T(8,128)(2,1)S(1)}, bf16[128,4096]{1,0:T(8,128)(2,1)S(1)}, u32[]{:S(2)}, u32[]{:S(2)}) collective-permute-start(bf16[128,4096]{1,0:T(8,128)(2,1)S(1)} %get-tuple-element.36.refs_0_.p_ref), channel_id=1, source_target_pairs={{1,6},{3,0},{5,2},{7,4},{9,14},{11,8},{13,10},{15,12},{17,22},{19,... | collective-permute-start | bytes 3145736 | tf_op jit(solution)/shard_map/ppermute | solution.py:247
  13.5 6.7 %collective-permute-done.source = bf16[128,4096]{1,0:T(8,128)(2,1)S(1)} collective-permute-done((bf16[128,4096]{1,0:T(8,128)(2,1)}, bf16[128,4096]{1,0:T(8,128)(2,1)S(1)}, u32[]{:S(2)}, u32[]{:S(2)}) %collective-permute-start) | collective-permute-done | bytes 1048608 | tf_op jit(solution)/shard_map/ppermute | solution.py:247
  20.3 0.7 collective-permute-start.3
  21.0 7.3 %collective-permute-done.1.refs_2_.e3_ref = bf16[128,4096]{1,0:T(8,128)(2,1)S(1)} collective-permute-done((bf16[128,4096]{1,0:T(8,128)(2,1)S(1)}, bf16[128,4096]{1,0:T(8,128)(2,1)S(1)}, u32[]{:S(2)}, u32[]{:S(2)}) %collective-permute-start.1) | collective-permute-done | bytes 1048608 | tf_op jit(solution)/shard_map/ppermute | solution.py:247
  28.4 0.8 collective-permute-start.2
  29.2 1.0 %shard_map.69 = (f32[128,128]{1,0:T(8,128)S(1)}, f32[128,128]{1,0:T(8,128)S(1)}, f32[128,128]{1,0:T(8,128)S(1)}) custom-call(bf16[128,4096]{1,0:T(8,128)(2,1)S(1)} %get-tuple-element.35.q_ref, bf16[128,4096]{1,0:T(8,128)(2,1)S(1)} %get-tuple-element.36.refs_0_.p_ref, bf16[128,4096]{1,0:T(8,128)(2,1)S(1)} %shard_map.68.refs_1_.n1_ref, ...), custom_call_target="tpu_custom_call" | custom-call | bytes 4390912 | tf_op jit(solution)/shard_map/pallas_call | solution.py:31
  30.2 3.7 %collective-permute-done.5.refs_2_ = bf16[272,1024]{1,0:T(8,128)(2,1)S(1)} collective-permute-done((bf16[272,1024]{1,0:T(8,128)(2,1)S(1)}, bf16[272,1024]{1,0:T(8,128)(2,1)S(1)}, u32[]{:S(2)}, u32[]{:S(2)}) %collective-permute-start.5) | collective-permute-done | bytes 557088 | tf_op jit(solution)/shard_map/ppermute | solution.py:255
  33.9 1.4 %shard_map.72 = (f32[3,128]{1,0:T(4,128)S(1)}, f32[3,128]{1,0:T(4,128)S(1)}, f32[3,128]{1,0:T(4,128)S(1)}, f32[3,128]{1,0:T(4,128)S(1)}) custom-call(bf16[272,1024]{1,0:T(8,128)(2,1)S(1)} %get-tuple-element.41.refs_0_, bf16[272,1024]{1,0:T(8,128)(2,1)S(1)} %collective-permute-done.4.refs_1_, bf16[272,1024]{1,0:T(8,128)(2,1)S(1)} %collective-permute-done.5.refs_2_, ...), custom_call_target="tpu_custom_call" | custom-call | flops 49999998976 | bytes 2299904 | tf_op jit(solution)/shard_map/pallas_call | solution.py:31
  35.3 1.3 %collective-permute-start.7 = (f32[3,128]{1,0:T(4,128)S(1)}, f32[3,128]{1,0:T(4,128)S(1)}, u32[]{:S(2)}, u32[]{:S(2)}) collective-permute-start(f32[3,128]{1,0:T(4,128)S(1)} %get-tuple-element.46), channel_id=1, source_target_pairs={{0,8},{8,0},{16,24},{24,16},{1,9},{9,1},{17,25},{25,17},{2,10},{10... | collective-permute-start | bytes 4616 | tf_op jit(solution)/shard_map/ppermute | solution.py:255
  36.6 0.8 collective-permute-start.8
  37.5 1.4 %collective-permute-start.9 = (f32[3,128]{1,0:T(4,128)S(1)}, f32[3,128]{1,0:T(4,128)S(1)}, u32[]{:S(2)}, u32[]{:S(2)}) collective-permute-start(f32[3,128]{1,0:T(4,128)S(1)} %get-tuple-element.48), channel_id=1, source_target_pairs={{0,24},{8,16},{16,8},{24,0},{1,25},{9,17},{17,9},{25,1},{2,26},{10... | collective-permute-start | bytes 4616 | tf_op jit(solution)/shard_map/ppermute | solution.py:255
  39.4 0.9 %collective-permute-done.8.refs_2_ = f32[3,128]{1,0:T(4,128)S(1)} collective-permute-done((f32[3,128]{1,0:T(4,128)S(1)}, f32[3,128]{1,0:T(4,128)S(1)}, u32[]{:S(2)}, u32[]{:S(2)}) %collective-permute-start.8) | collective-permute-done | bytes 1568 | tf_op jit(solution)/shard_map/ppermute | solution.py:255
  40.2 1.7 %collective-permute-done.9.refs_3_ = f32[3,128]{1,0:T(4,128)S(1)} collective-permute-done((f32[3,128]{1,0:T(4,128)S(1)}, f32[3,128]{1,0:T(4,128)S(1)}, u32[]{:S(2)}, u32[]{:S(2)}) %collective-permute-start.9) | collective-permute-done | bytes 1568 | tf_op jit(solution)/shard_map/ppermute | solution.py:255
  42.0 1.2 %shard_map.73 = (f32[1,128]{1,0:T(1,128)}, bf16[512,128]{1,0:T(8,128)(2,1)S(1)}, f32[3,128]{1,0:T(4,128)S(1)}, bf16[128,4096]{1,0:T(8,128)(2,1)S(1)}, bf16[128,4096]{1,0:T(8,128)(2,1)S(1)}) custom-call(bf16[128,4096]{1,0:T(8,128)(2,1)S(1)} %get-tuple-element.35.q_ref, f32[128,128]{1,0:T(8,128)S(1)} %get-tuple-element.38.refs_4_.s0_ref, ...), custom_call_target="tpu_custom_call" | custom-call | bytes 4596224 | tf_op jit(solution)/shard_map/pallas_call | solution.py:31
  44.0 1.5 %collective-permute-start.14 = (f32[3,128]{1,0:T(4,128)S(1)}, f32[3,128]{1,0:T(4,128)S(1)}, u32[]{:S(2)}, u32[]{:S(2)}) collective-permute-start(f32[3,128]{1,0:T(4,128)S(1)} %get-tuple-element.54.refs_4_), channel_id=1, source_target_pairs={{0,24},{8,16},{16,8},{24,0},{1,25},{9,17},{17,9},{25,1},{2,26},{10... | collective-permute-start | bytes 4616 | tf_op jit(solution)/shard_map/ppermute | solution.py:255
  45.5 1.5 %collective-permute-start.13 = (f32[3,128]{1,0:T(4,128)S(1)}, f32[3,128]{1,0:T(4,128)S(1)}, u32[]{:S(2)}, u32[]{:S(2)}) collective-permute-start(f32[3,128]{1,0:T(4,128)S(1)} %get-tuple-element.54.refs_4_), channel_id=1, source_target_pairs={{0,16},{8,24},{16,0},{24,8},{1,17},{9,25},{17,1},{25,9},{2,18},{10... | collective-permute-start | bytes 4616 | tf_op jit(solution)/shard_map/ppermute | solution.py:255
  47.8 0.7 collective-permute-done.14.refs_7_
  49.1 1.5 %collective-permute-done.12.refs_5_ = f32[3,128]{1,0:T(4,128)S(1)} collective-permute-done((f32[3,128]{1,0:T(4,128)S(1)}, f32[3,128]{1,0:T(4,128)S(1)}, u32[]{:S(2)}, u32[]{:S(2)}) %collective-permute-start.12) | collective-permute-done | bytes 1568 | tf_op jit(solution)/shard_map/ppermute | solution.py:255
  50.6 1.5 %shard_map.75 = (bf16[256,1024]{1,0:T(8,128)(2,1)S(1)}, bf16[256,1024]{1,0:T(8,128)(2,1)S(1)}, bf16[256,1024]{1,0:T(8,128)(2,1)S(1)}, bf16[256,1024]{1,0:T(8,128)(2,1)S(1)}, f32[8,128]{1,0:T(8,128)S(1)}) custom-call(bf16[272,1024]{1,0:T(8,128)(2,1)S(1)} %get-tuple-element.41.refs_0_, bf16[272,1024]{1,0:T(8,128)(2,1)S(1)} %collective-permute-done.4.refs_1_, ...), custom_call_target="tpu_custom_call" | custom-call | bytes 4339712 | tf_op jit(solution)/shard_map/pallas_call | solution.py:31
  52.8 1.2 %collective-permute-start.18 = (bf16[256,1024]{1,0:T(8,128)(2,1)S(1)}, bf16[256,1024]{1,0:T(8,128)(2,1)S(1)}, u32[]{:S(2)}, u32[]{:S(2)}) collective-permute-start(bf16[256,1024]{1,0:T(8,128)(2,1)S(1)} %get-tuple-element.63), channel_id=1, source_target_pairs={{0,16},{8,24},{16,0},{24,8},{1,17},{9,25},{17,1},{25,9},{2,18},{10... | collective-permute-start | bytes 1572872 | tf_op jit(solution)/shard_map/ppermute | solution.py:255
  54.0 1.8 %collective-permute-start.19 = (bf16[256,1024]{1,0:T(8,128)(2,1)S(1)}, bf16[256,1024]{1,0:T(8,128)(2,1)S(1)}, u32[]{:S(2)}, u32[]{:S(2)}) collective-permute-start(bf16[256,1024]{1,0:T(8,128)(2,1)S(1)} %get-tuple-element.64), channel_id=1, source_target_pairs={{0,24},{8,16},{16,8},{24,0},{1,25},{9,17},{17,9},{25,1},{2,26},{10... | collective-permute-start | bytes 1572872 | tf_op jit(solution)/shard_map/ppermute | solution.py:255
  55.7 3.6 %collective-permute-start.11 = (bf16[128,4096]{1,0:T(8,128)(2,1)S(1)}, bf16[128,4096]{1,0:T(8,128)(2,1)S(1)}, u32[]{:S(2)}, u32[]{:S(2)}) collective-permute-start(bf16[128,4096]{1,0:T(8,128)(2,1)S(1)} %get-tuple-element.53), channel_id=1, source_target_pairs={{0,3},{2,5},{4,7},{6,1},{8,11},{10,13},{12,15},{14,9},{16,19},{18,... | collective-permute-start | bytes 3145736 | tf_op jit(solution)/shard_map/ppermute | solution.py:247
  59.9 1.5 %collective-permute-start.16 = (bf16[128,4096]{1,0:T(8,128)(2,1)S(1)}, bf16[128,4096]{1,0:T(8,128)(2,1)S(1)}, u32[]{:S(2)}, u32[]{:S(2)}) collective-permute-start(bf16[128,4096]{1,0:T(8,128)(2,1)S(1)} %get-tuple-element.60), channel_id=1, source_target_pairs={{0,1},{1,2},{2,3},{3,4},{4,5},{5,6},{6,7},{7,0},{8,9},{9,10},{10,1... | collective-permute-start | bytes 3145736 | tf_op jit(solution)/shard_map/ppermute | solution.py:247
  61.4 19.5 %collective-permute-done.11.own3_ref = bf16[128,4096]{1,0:T(8,128)(2,1)S(1)} collective-permute-done((bf16[128,4096]{1,0:T(8,128)(2,1)S(1)}, bf16[128,4096]{1,0:T(8,128)(2,1)S(1)}, u32[]{:S(2)}, u32[]{:S(2)}) %collective-permute-start.11) | collective-permute-done | bytes 1048608 | tf_op jit(solution)/shard_map/ppermute | solution.py:247
  80.9 1.5 %shard_map.78 = (f32[128,4096]{1,0:T(8,128)S(1)}, f32[128,4096]{1,0:T(8,128)S(1)}) custom-call(bf16[128,4096]{1,0:T(8,128)(2,1)S(1)} %get-tuple-element.35.q_ref, bf16[128,4096]{1,0:T(8,128)(2,1)S(1)} %get-tuple-element.36.refs_0_.p_ref, bf16[128,4096]{1,0:T(8,128)(2,1)S(1)} %shard_map.68.refs_1_.n1_ref, ...), custom_call_target="tpu_custom_call" | custom-call | flops 49999998976 | bytes 11670016 | tf_op jit(solution)/shard_map/pallas_call | solution.py:31
  82.4 3.0 %collective-permute-done.16.own1 = bf16[128,4096]{1,0:T(8,128)(2,1)S(1)} collective-permute-done((bf16[128,4096]{1,0:T(8,128)(2,1)S(1)}, bf16[128,4096]{1,0:T(8,128)(2,1)S(1)}, u32[]{:S(2)}, u32[]{:S(2)}) %collective-permute-start.16) | collective-permute-done | bytes 1048608 | tf_op jit(solution)/shard_map/ppermute | solution.py:247
  85.4 1.5 %shard_map.79 = (bf16[128,4096]{1,0:T(8,128)(2,1)}, bf16[128,4096]{1,0:T(8,128)(2,1)}) custom-call(f32[128,4096]{1,0:T(8,128)S(1)} %get-tuple-element.58.pulled, f32[128,4096]{1,0:T(8,128)S(1)} %get-tuple-element.59.base, bf16[128,4096]{1,0:T(8,128)(2,1)S(1)} %collective-permute-done.16.own1, bf16[256,1024]{1,0:T(8,128)(2,1)S(1)} %get-tuple-element.61.refs_0_, ...), custom_call_target="tpu_custom_call" | custom-call | bytes 9437184 | tf_op jit(solution)/shard_map/pallas_call | solution.py:31
  (29 shorter events, 5.5 us)
Async XLA Ops:
  0.6 19.6 %collective-permute-start = (bf16[128,4096]{1,0:T(8,128)(2,1)}, bf16[128,4096]{1,0:T(8,128)(2,1)S(1)}, u32[]{:S(2)}, u32[]{:S(2)}) collective-permute-start(bf16[128,4096]{1,0:T(8,128)(2,1)} %p_hbm.1), channel_id=1, source_target_pairs={{0,7},{1,0},{2,1},{3,2},{4,3},{5,4},{6,5},{7,6},{8,15},{9,8},{10,9... | collective-permute-start | bytes 3145736 | tf_op jit(solution)/shard_map/ppermute | solution.py:247
  5.2 1.2 %copy-start = (bf16[128,4096]{1,0:T(8,128)(2,1)S(1)}, bf16[128,4096]{1,0:T(8,128)(2,1)}, u32[]{:S(2)}) copy-start(bf16[128,4096]{1,0:T(8,128)(2,1)} %q_hbm.1) | copy-start | bytes 3145732
  6.4 1.2 %copy-start.1 = (bf16[128,4096]{1,0:T(8,128)(2,1)S(1)}, bf16[128,4096]{1,0:T(8,128)(2,1)}, u32[]{:S(2)}) copy-start(bf16[128,4096]{1,0:T(8,128)(2,1)} %p_hbm.1) | copy-start | bytes 3145732
  7.6 0.7 copy-start.2
  8.7 21.5 %collective-permute-start.4 = (bf16[272,1024]{1,0:T(8,128)(2,1)S(1)}, bf16[272,1024]{1,0:T(8,128)(2,1)S(1)}, u32[]{:S(2)}, u32[]{:S(2)}) collective-permute-start(bf16[272,1024]{1,0:T(8,128)(2,1)S(1)} %get-tuple-element.42), channel_id=1, source_target_pairs={{0,8},{8,0},{16,24},{24,16},{1,9},{9,1},{17,25},{25,17},{2,10},{10... | collective-permute-start | bytes 1671176 | tf_op jit(solution)/shard_map/ppermute | solution.py:255
  10.2 23.7 %collective-permute-start.5 = (bf16[272,1024]{1,0:T(8,128)(2,1)S(1)}, bf16[272,1024]{1,0:T(8,128)(2,1)S(1)}, u32[]{:S(2)}, u32[]{:S(2)}) collective-permute-start(bf16[272,1024]{1,0:T(8,128)(2,1)S(1)} %get-tuple-element.43), channel_id=1, source_target_pairs={{0,16},{8,24},{16,0},{24,8},{1,17},{9,25},{17,1},{25,9},{2,18},{10... | collective-permute-start | bytes 1671176 | tf_op jit(solution)/shard_map/ppermute | solution.py:255
  11.8 22.1 %collective-permute-start.6 = (bf16[272,1024]{1,0:T(8,128)(2,1)S(1)}, bf16[272,1024]{1,0:T(8,128)(2,1)S(1)}, u32[]{:S(2)}, u32[]{:S(2)}) collective-permute-start(bf16[272,1024]{1,0:T(8,128)(2,1)S(1)} %get-tuple-element.44), channel_id=1, source_target_pairs={{0,24},{8,16},{16,8},{24,0},{1,25},{9,17},{17,9},{25,1},{2,26},{10... | collective-permute-start | bytes 1671176 | tf_op jit(solution)/shard_map/ppermute | solution.py:255
  12.2 16.1 %collective-permute-start.1 = (bf16[128,4096]{1,0:T(8,128)(2,1)S(1)}, bf16[128,4096]{1,0:T(8,128)(2,1)S(1)}, u32[]{:S(2)}, u32[]{:S(2)}) collective-permute-start(bf16[128,4096]{1,0:T(8,128)(2,1)S(1)} %get-tuple-element.36.refs_0_.p_ref), channel_id=1, source_target_pairs={{1,6},{3,0},{5,2},{7,4},{9,14},{11,8},{13,10},{15,12},{17,22},{19,... | collective-permute-start | bytes 3145736 | tf_op jit(solution)/shard_map/ppermute | solution.py:247
  20.3 21.7 %collective-permute-start.3 = (bf16[128,4096]{1,0:T(8,128)(2,1)S(1)}, bf16[128,4096]{1,0:T(8,128)(2,1)S(1)}, u32[]{:S(2)}, u32[]{:S(2)}) collective-permute-start(bf16[128,4096]{1,0:T(8,128)(2,1)S(1)} %shard_map.68.refs_1_.n1_ref), channel_id=1, source_target_pairs={{1,7},{3,1},{5,3},{7,5},{9,15},{11,9},{13,11},{15,13},{17,23},{19,... | collective-permute-start | bytes 3145736 | tf_op jit(solution)/shard_map/ppermute | solution.py:247
  28.4 10.5 %collective-permute-start.2 = (bf16[128,4096]{1,0:T(8,128)(2,1)S(1)}, bf16[128,4096]{1,0:T(8,128)(2,1)S(1)}, u32[]{:S(2)}, u32[]{:S(2)}) collective-permute-start(bf16[128,4096]{1,0:T(8,128)(2,1)S(1)} %shard_map.70), channel_id=1, source_target_pairs={{0,1},{1,0},{2,3},{3,2},{4,5},{5,4},{6,7},{7,6},{8,9},{9,8},{10,11... | collective-permute-start | bytes 3145736 | tf_op jit(solution)/shard_map/ppermute | solution.py:250
  35.3 6.6 %copy-start.3 = (f32[128]{0:T(128)S(1)}, f32[128]{0:T(128)}, u32[]{:S(2)}) copy-start(f32[128]{0:T(128)} %param.7) | copy-start | bytes 1540
  35.3 4.0 %collective-permute-start.7 = (f32[3,128]{1,0:T(4,128)S(1)}, f32[3,128]{1,0:T(4,128)S(1)}, u32[]{:S(2)}, u32[]{:S(2)}) collective-permute-start(f32[3,128]{1,0:T(4,128)S(1)} %get-tuple-element.46), channel_id=1, source_target_pairs={{0,8},{8,0},{16,24},{24,16},{1,9},{9,1},{17,25},{25,17},{2,10},{10... | collective-permute-start | bytes 4616 | tf_op jit(solution)/shard_map/ppermute | solution.py:255
  36.6 3.6 %collective-permute-start.8 = (f32[3,128]{1,0:T(4,128)S(1)}, f32[3,128]{1,0:T(4,128)S(1)}, u32[]{:S(2)}, u32[]{:S(2)}) collective-permute-start(f32[3,128]{1,0:T(4,128)S(1)} %get-tuple-element.47), channel_id=1, source_target_pairs={{0,16},{8,24},{16,0},{24,8},{1,17},{9,25},{17,1},{25,9},{2,18},{10... | collective-permute-start | bytes 4616 | tf_op jit(solution)/shard_map/ppermute | solution.py:255
  37.5 4.5 %collective-permute-start.9 = (f32[3,128]{1,0:T(4,128)S(1)}, f32[3,128]{1,0:T(4,128)S(1)}, u32[]{:S(2)}, u32[]{:S(2)}) collective-permute-start(f32[3,128]{1,0:T(4,128)S(1)} %get-tuple-element.48), channel_id=1, source_target_pairs={{0,24},{8,16},{16,8},{24,0},{1,25},{9,17},{17,9},{25,1},{2,26},{10... | collective-permute-start | bytes 4616 | tf_op jit(solution)/shard_map/ppermute | solution.py:255
  43.2 4.4 %collective-permute-start.10 = (bf16[128,4096]{1,0:T(8,128)(2,1)S(1)}, bf16[128,4096]{1,0:T(8,128)(2,1)S(1)}, u32[]{:S(2)}, u32[]{:S(2)}) collective-permute-start(bf16[128,4096]{1,0:T(8,128)(2,1)S(1)} %get-tuple-element.52), channel_id=1, source_target_pairs={{0,1},{1,0},{2,3},{3,2},{4,5},{5,4},{6,7},{7,6},{8,9},{9,8},{10,11... | collective-permute-start | bytes 3145736 | tf_op jit(solution)/shard_map/ppermute | solution.py:250
  43.3 16.4 %collective-permute-start.15 = (bf16[128,4096]{1,0:T(8,128)(2,1)S(1)}, bf16[128,4096]{1,0:T(8,128)(2,1)S(1)}, u32[]{:S(2)}, u32[]{:S(2)}) collective-permute-start(bf16[128,4096]{1,0:T(8,128)(2,1)S(1)} %get-tuple-element.51.a_ref), channel_id=1, source_target_pairs={{1,3},{3,5},{5,7},{7,1},{9,11},{11,13},{13,15},{15,9},{17,19},{19,... | collective-permute-start | bytes 3145736 | tf_op jit(solution)/shard_map/ppermute | solution.py:247
  44.0 4.5 %collective-permute-start.14 = (f32[3,128]{1,0:T(4,128)S(1)}, f32[3,128]{1,0:T(4,128)S(1)}, u32[]{:S(2)}, u32[]{:S(2)}) collective-permute-start(f32[3,128]{1,0:T(4,128)S(1)} %get-tuple-element.54.refs_4_), channel_id=1, source_target_pairs={{0,24},{8,16},{16,8},{24,0},{1,25},{9,17},{17,9},{25,1},{2,26},{10... | collective-permute-start | bytes 4616 | tf_op jit(solution)/shard_map/ppermute | solution.py:255
  45.5 3.6 %collective-permute-start.13 = (f32[3,128]{1,0:T(4,128)S(1)}, f32[3,128]{1,0:T(4,128)S(1)}, u32[]{:S(2)}, u32[]{:S(2)}) collective-permute-start(f32[3,128]{1,0:T(4,128)S(1)} %get-tuple-element.54.refs_4_), channel_id=1, source_target_pairs={{0,16},{8,24},{16,0},{24,8},{1,17},{9,25},{17,1},{25,9},{2,18},{10... | collective-permute-start | bytes 4616 | tf_op jit(solution)/shard_map/ppermute | solution.py:255
  47.0 3.6 %collective-permute-start.12 = (f32[3,128]{1,0:T(4,128)S(1)}, f32[3,128]{1,0:T(4,128)S(1)}, u32[]{:S(2)}, u32[]{:S(2)}) collective-permute-start(f32[3,128]{1,0:T(4,128)S(1)} %get-tuple-element.54.refs_4_), channel_id=1, source_target_pairs={{0,8},{8,0},{16,24},{24,16},{1,9},{9,1},{17,25},{25,17},{2,10},{10... | collective-permute-start | bytes 4616 | tf_op jit(solution)/shard_map/ppermute | solution.py:255
  52.2 30.2 %collective-permute-start.17 = (bf16[256,1024]{1,0:T(8,128)(2,1)S(1)}, bf16[256,1024]{1,0:T(8,128)(2,1)S(1)}, u32[]{:S(2)}, u32[]{:S(2)}) collective-permute-start(bf16[256,1024]{1,0:T(8,128)(2,1)S(1)} %get-tuple-element.62), channel_id=1, source_target_pairs={{0,8},{8,0},{16,24},{24,16},{1,9},{9,1},{17,25},{25,17},{2,10},{10... | collective-permute-start | bytes 1572872 | tf_op jit(solution)/shard_map/ppermute | solution.py:255
  52.8 29.6 %collective-permute-start.18 = (bf16[256,1024]{1,0:T(8,128)(2,1)S(1)}, bf16[256,1024]{1,0:T(8,128)(2,1)S(1)}, u32[]{:S(2)}, u32[]{:S(2)}) collective-permute-start(bf16[256,1024]{1,0:T(8,128)(2,1)S(1)} %get-tuple-element.63), channel_id=1, source_target_pairs={{0,16},{8,24},{16,0},{24,8},{1,17},{9,25},{17,1},{25,9},{2,18},{10... | collective-permute-start | bytes 1572872 | tf_op jit(solution)/shard_map/ppermute | solution.py:255
  54.0 28.5 %collective-permute-start.19 = (bf16[256,1024]{1,0:T(8,128)(2,1)S(1)}, bf16[256,1024]{1,0:T(8,128)(2,1)S(1)}, u32[]{:S(2)}, u32[]{:S(2)}) collective-permute-start(bf16[256,1024]{1,0:T(8,128)(2,1)S(1)} %get-tuple-element.64), channel_id=1, source_target_pairs={{0,24},{8,16},{16,8},{24,0},{1,25},{9,17},{17,9},{25,1},{2,26},{10... | collective-permute-start | bytes 1572872 | tf_op jit(solution)/shard_map/ppermute | solution.py:255
  55.7 25.2 %collective-permute-start.11 = (bf16[128,4096]{1,0:T(8,128)(2,1)S(1)}, bf16[128,4096]{1,0:T(8,128)(2,1)S(1)}, u32[]{:S(2)}, u32[]{:S(2)}) collective-permute-start(bf16[128,4096]{1,0:T(8,128)(2,1)S(1)} %get-tuple-element.53), channel_id=1, source_target_pairs={{0,3},{2,5},{4,7},{6,1},{8,11},{10,13},{12,15},{14,9},{16,19},{18,... | collective-permute-start | bytes 3145736 | tf_op jit(solution)/shard_map/ppermute | solution.py:247
  59.9 25.5 %collective-permute-start.16 = (bf16[128,4096]{1,0:T(8,128)(2,1)S(1)}, bf16[128,4096]{1,0:T(8,128)(2,1)S(1)}, u32[]{:S(2)}, u32[]{:S(2)}) collective-permute-start(bf16[128,4096]{1,0:T(8,128)(2,1)S(1)} %get-tuple-element.60), channel_id=1, source_target_pairs={{0,1},{1,2},{2,3},{3,4},{4,5},{5,6},{6,7},{7,0},{8,9},{9,10},{10,1... | collective-permute-start | bytes 3145736 | tf_op jit(solution)/shard_map/ppermute | solution.py:247
where the time goes:
time: 87.3 us; the launch traced here: 87 us
  waiting for transfers between devices  45.7 us (52%)
  starting transfers between devices  27.4 us (31%)
  Pallas kernels  9.96 us (11%)
  local copies, waits for them, and re-layouts  3.14 us (4%)
    ppermute x6, waiting for transfers between devices, shift(): return lax.ppermute(array, 'blk', pairs)  36.5 us
    ppermute x12, starting transfers between devices, exchange(): out[r] = lax.ppermute(arrays[r], 'grp', [(i, i ^ r) for i in range(groups)])  14.2 us
    ppermute x6, starting transfers between devices, shift(): return lax.ppermute(array, 'blk', pairs)  12.3 us
    pallas_call x13, Pallas kernels, local_call(): pl.pallas_call(body, out_shape=out_shape, in_specs=in_specs or [VMEM] * l...  9.96 us
    ppermute x12, waiting for transfers between devices, exchange(): out[r] = lax.ppermute(arrays[r], 'grp', [(i, i ^ r) for i in range(groups)])  9.13 us
    unnamed x8, local copies, waits for them, and re-layouts  3.14 us
  transfers between devices with their start and end apart: 20, of which 10 were waited for; matrix products, arithmetic and copies ran while one was open for 0% of the time, Pallas kernels for 8%

commit v1 on v0

--- a/solution.py
+++ b/solution.py
@@ -13,7 +13,7 @@
 F32 = jnp.float32
 CHUNK = 512
 TAIL = 16
-LONG, SOME = 5 * 10**10, 16 * 10**9
+LONG = 5 * 10**10
 VMEM = pl.BlockSpec(memory_space=pltpu.VMEM)
 HBM = pl.BlockSpec(memory_space=pltpu.HBM)
 TOKEN = jax.ShapeDtypeStruct((8, 128), F32)
@@ -87,8 +87,8 @@
     return [(tail[k : k + 1, :rows] ^ g) * rows + tail[k : k + 1, rows:] for k in range(3)]
 
 
-def hard_scores_body(groups, *refs):
-    pieces, outs = refs[:groups], refs[groups + 1 :]
+def hard_scores_body(groups, q_ref, *refs):
+    pieces, outs, later = refs[:groups], refs[groups + 1 : -1], refs[-1]
     rows = outs[0].shape[1]
     ids = lax.broadcasted_iota(jnp.int32, (groups * rows, rows), 0)
     p_all = jnp.concatenate([piece[rows : 2 * rows] for piece in pieces], axis=0)
@@ -98,13 +98,15 @@
         for k in range(3):
             hit = jnp.where(ids == places[k], dots, 0.0)
             outs[r][k : k + 1] = jnp.sum(hit, axis=0, keepdims=True)
+    later[...] = q_ref[...]
 
 
 def hard_grads_body(groups, *refs):
-    pieces, coefs, outs = refs[:groups], refs[groups : 2 * groups], refs[2 * groups + 1 : 3 * groups + 1]
-    token, matrix, matrix_t = refs[3 * groups + 1 :]
+    pieces, coefs, out = refs[:groups], refs[groups : 2 * groups], refs[2 * groups]
+    token, matrix, matrix_t = refs[2 * groups + 1 :]
     rows = coefs[0].shape[1]
-    cols = outs[0].shape[1]
+    cols = out.shape[2]
+    g = lax.axis_index("grp")
     signal(token)
     ids = lax.broadcasted_iota(jnp.int32, (groups * rows, rows), 0)
     for r in range(groups):
@@ -124,24 +126,24 @@
         grad_p = dot(matrix[...], q_all, ((1,), (0,))).astype(BF16)
         for r in range(groups):
             mine = slice(r * rows, (r + 1) * rows)
-            outs[r][:rows, at] = grad_q[mine]
-            outs[r][rows:, at] = grad_p[mine]
+            out[g ^ r, :rows, at] = grad_q[mine]
+            out[g ^ r, rows:, at] = grad_p[mine]
 
 
 def pass_body(source, token, out):
     out[...] = source[...]
 
 
-def choose_body(n1_ref, e3_ref, out):
-    odd = lax.axis_index("blk") % 2 == 1
-
-    @pl.when(odd)
+def choose_body(parity, first_ref, second_ref, out):
+    here = lax.axis_index("blk") % 2 == parity
+
+    @pl.when(here)
     def _():
-        out[...] = n1_ref[...]
-
-    @pl.when(jnp.logical_not(odd))
+        out[...] = first_ref[...]
+
+    @pl.when(jnp.logical_not(here))
     def _():
-        out[...] = e3_ref[...]
+        out[...] = second_ref[...]
 
 
 def scores_body(q_ref, *refs):
@@ -151,14 +153,14 @@
 
 
 def weigh_body(groups, q_ref, s0_ref, s1_ref, s2_ref, s3_ref, last_ref, w_ref, *refs):
-    hard_refs = refs[:groups]
-    loss_ref, coef_ref, hard_out, term3_ref, term2_ref = refs[groups:]
-    rows, width = q_ref.shape
+    parts = refs[:groups]
+    loss_ref, hard_out, *coef_refs = refs[groups:]
+    rows = q_ref.shape[0]
     w = w_ref[...]
     s3 = INV_TEMP * (s3_ref[...] + dot(last_ref[...], q_ref[...], ((1,), (1,))))
     scores = [INV_TEMP * s0_ref[...], INV_TEMP * s1_ref[...], INV_TEMP * s2_ref[...], s3]
-    hard = hard_refs[0][...]
-    for other in hard_refs[1:]:
+    hard = parts[0][...]
+    for other in parts[1:]:
         hard = hard + other[...]
     hard = INV_TEMP * hard
     largest = jnp.max(hard, axis=0, keepdims=True)
@@ -168,68 +170,57 @@
     for block in scores:
         summed = summed + jnp.sum(jnp.exp(block - largest), axis=0, keepdims=True)
     log_total = largest + jnp.log(summed)
-    for s in range(4):
-        coef_ref[s * rows : (s + 1) * rows] = (w * jnp.exp(scores[s] - log_total)).astype(BF16)
-    for c in range(0, width, CHUNK):
-        at = slice(c, c + CHUNK)
-        both = dot(coef_ref[2 * rows :], q_ref[:, at], ((1,), (0,))).astype(BF16)
-        term2_ref[:, at] = both[:rows]
-        term3_ref[:, at] = both[rows:]
     hard_out[...] = (w * jnp.exp(hard - log_total)).astype(BF16).astype(F32)
+    for block, coef_ref in zip(scores, coef_refs):
+        coef_ref[...] = (w * jnp.exp(block - log_total)).astype(BF16)
     eye = lax.broadcasted_iota(jnp.int32, (rows, rows), 0) == lax.broadcasted_iota(
         jnp.int32, (rows, rows), 1
     )
     loss_ref[...] = log_total - jnp.sum(jnp.where(eye, scores[0], 0.0), axis=0, keepdims=True)
 
 
-def add_body(a_ref, b_ref, out, token):
-    signal(token)
-    out[...] = (a_ref[...].astype(F32) + b_ref[...].astype(F32)).astype(BF16)
-
-
-def term1_body(q_ref, coef_ref, got2_ref, token, out):
-    rows, width = q_ref.shape
-    keep = jnp.where(lax.axis_index("blk") % 2 == 1, 1.0, 0.0)
-    for c in range(0, width, CHUNK):
-        at = slice(c, c + CHUNK)
-        term1 = dot(coef_ref[rows : 2 * rows], q_ref[:, at], ((1,), (0,)))
-        out[:, at] = term1 + keep * got2_ref[:, at].astype(F32)
-
-
-def relay_body(partial1, got3_ref, out, done):
-    signal(done)
-    out[...] = (partial1[...] + got3_ref[...].astype(F32)).astype(BF16)
-
-
-def base_body(
-    q_ref, p_ref, n1_ref, n2_ref, e3_ref, o3_ref, coef_ref, w_ref, own3_ref, token, pulled, base
-):
-    rows, width = q_ref.shape
-    w = jnp.broadcast_to(w_ref[...], (rows, rows)).T[:, :1]
+def column(row_ref, rows):
+    return jnp.broadcast_to(row_ref[...], (rows, rows)).T[:, :1]
+
+
+def queries_body(p_ref, n1_ref, n2_ref, e3_ref, o3_ref, w_ref, *refs):
+    coefs, pulled, sent, coef_t = refs[:4], refs[5], refs[6:9], refs[9]
+    for coef, out in zip(coefs[1:], sent):
+        out[...] = coef[...]
+    rows, width = p_ref.shape
+    w = column(w_ref, rows)
+    for s in range(5):
+        coef_t[:, s * rows : (s + 1) * rows] = coefs[min(s, 3)][...].astype(F32).T.astype(BF16)
     blocks = (p_ref, n1_ref, n2_ref, e3_ref, o3_ref)
-    coef_t = coef_ref[...].astype(F32).T.astype(BF16)
-    coef_t = jnp.concatenate([coef_t, coef_t[:, 3 * rows :]], axis=1)
     for c in range(0, width, CHUNK):
         at = slice(c, c + CHUNK)
         held = jnp.concatenate([block[:, at] for block in blocks], axis=0)
-        pulled[:, at] = dot(coef_t, held, ((1,), (0,))) - w * p_ref[:, at].astype(F32)
-        own = dot(coef_ref[:rows], q_ref[:, at], ((1,), (0,))) + own3_ref[:, at].astype(F32)
-        base[:, at] = own - w * q_ref[:, at].astype(F32)
-
-
-def finish_body(groups, pulled, base, own1, *refs):
-    backs = refs[:groups]
-    q_out, p_out, q_held, p_held, sems = refs[groups:]
-    rows, cols = pulled.shape[0], backs[0].shape[1]
-    g = lax.axis_index("grp")
+        pulled[:, at] = dot(coef_t[...], held, ((1,), (0,))) - w * p_ref[:, at].astype(F32)
+
+
+def passages_body(q_ref, m1_ref, m2_ref, u3_ref, w_ref, *refs):
+    coefs, base = refs[:4], refs[-1]
+    rows, width = q_ref.shape
+    w = column(w_ref, rows)
+    coef = jnp.concatenate([coef[...] for coef in coefs], axis=1)
+    for c in range(0, width, CHUNK):
+        at = slice(c, c + CHUNK)
+        held = jnp.concatenate([ref[:, at] for ref in (q_ref, m1_ref, m2_ref, u3_ref)], axis=0)
+        base[:, at] = dot(coef, held, ((1,), (0,))) - w * q_ref[:, at].astype(F32)
+
+
+def finish_body(groups, pulled, base, r3_ref, coef3, *refs):
+    backs, q_out, p_out, q_held, p_held, sems = refs
+    rows, cols = pulled.shape[0], backs.shape[2]
     copies = []
-    for r, back in enumerate(backs):
-        at = pl.ds(pl.multiple_of((g ^ r) * cols, 128), cols)
+    for r in range(groups):
+        back = backs.at[r]
+        at = slice(r * cols, (r + 1) * cols)
         q_held[:, at] = (INV_TEMP * (pulled[:, at] + back[:rows].astype(F32))).astype(BF16)
         copies.append(pltpu.make_async_copy(q_held.at[:, at], q_out.at[:, at], sems.at[2 * r]))
         copies[-1].start()
-        total = base[:, at] + back[rows:].astype(F32) + own1[:, at].astype(F32)
-        p_held[:, at] = (INV_TEMP * total).astype(BF16)
+        total = base[:, at] + dot(coef3[...], r3_ref[:, at], ((1,), (0,)))
+        p_held[:, at] = (INV_TEMP * (total + back[rows:].astype(F32))).astype(BF16)
         copies.append(pltpu.make_async_copy(p_held.at[:, at], p_out.at[:, at], sems.at[2 * r + 1]))
         copies[-1].start()
     for copy in copies:
@@ -259,8 +250,9 @@
         return jax.ShapeDtypeStruct(shape, dtype)
 
     block, block32 = like(rows, width), like(rows, width, dtype=F32)
-    square, triple = like(rows, rows, dtype=F32), like(3, rows, dtype=F32)
-    piece, back = like(2 * rows + TAIL, cols), like(2 * rows, cols)
+    square, square32 = like(rows, rows), like(rows, rows, dtype=F32)
+    row, triple = like(1, rows, dtype=F32), like(3, rows, dtype=F32)
+    piece, back = like(2 * rows + TAIL, cols), like(groups, 2 * rows, cols)
 
     next1 = shift(passages, -1)
 
@@ -276,46 +268,52 @@
     next3_even = shift(held_p, -3, (1,))
     (next1,) = local_call(pass_body, [block], next1, token, flops=LONG)
     next3_odd = shift(next1, -2, (1,))
-    next2 = swap(local_call(choose_body, [block], next1, next3_even, flops=LONG)[0])
-
-    s0, s1, s3 = local_call(scores_body, [square] * 3, held_q, held_p, next1, next3_even)
-    hard_parts = exchange(
-        local_call(
-            functools.partial(hard_scores_body, groups), [triple] * groups, *pieces, s0, flops=LONG
-        )
-    )
-    (s2,) = local_call(scores_body, [square], held_q, next2)
-    loss_rows, coef, hard_coef, term3, term2 = local_call(
-        functools.partial(weigh_body, groups),
-        [like(1, rows, dtype=F32), like(4 * rows, rows), triple, block, block],
-        held_q, s0, s1, s2, s3, next3_odd, weights[None, :], *hard_parts,
-    )
-
-    got3 = shift(term3, 2, (1,))
-    got2 = swap(term2)
-
-    sent3, token = local_call(add_body, [block, TOKEN], term3, got2)
-    own3 = shift(sent3, 3, (0,))
-
+    (held,) = local_call(
+        functools.partial(choose_body, 1), [block], next1, next3_even, flops=LONG
+    )
+    next2 = swap(held)
+
+    s0, s1, s3 = local_call(scores_body, [square32] * 3, held_q, held_p, next1, next3_even)
+    (s2,) = local_call(scores_body, [square32], held_q, next2)
+    *parts, later_q = local_call(
+        functools.partial(hard_scores_body, groups),
+        [triple] * groups + [block], held_q, *pieces, s0, flops=LONG,
+    )
+    parts = exchange(parts)
+    prev1 = shift(later_q, 1)
+    loss_rows, hard_coef, *coefs = local_call(
+        functools.partial(weigh_body, groups), [row, triple] + [square] * 4,
+        held_q, s0, s1, s2, s3, next3_odd, weights[None, :], *parts,
+    )
+
+    (later_q,) = local_call(pass_body, [block], held_q, hard_coef)
+    prev3_odd = shift(later_q, 3, (0,))
     hard_coefs = exchange([hard_coef] * groups)
-    square_all = pltpu.VMEM((groups * rows, groups * rows), BF16)
-    *backs, token = local_call(
-        functools.partial(hard_grads_body, groups), [back] * groups + [TOKEN],
-        *pieces, *hard_coefs, token, scratch=[square_all, square_all],
-    )
-    backs = exchange(backs)
-
-    (partial1,) = local_call(term1_body, [block32], held_q, coef, got2, token)
-    sent1, token = local_call(relay_body, [block, TOKEN], partial1, got3, flops=SOME)
-    own1 = shift(sent1, 1)
-
-    pulled, base = local_call(
-        base_body, [block32, block32],
-        held_q, held_p, next1, next2, next3_even, next3_odd, coef, weights[None, :], own3, token,
-        flops=LONG,
+    wide = pltpu.VMEM((groups * rows, groups * rows), BF16)
+    backs, token = local_call(
+        functools.partial(hard_grads_body, groups), [back, TOKEN],
+        *pieces, *hard_coefs, scratch=[wide, wide],
+    )
+    backs = lax.all_to_all(backs, "grp", split_axis=0, concat_axis=0, tiled=True)
+
+    (prev1,) = local_call(pass_body, [block], prev1, token)
+    prev3_even = shift(prev1, 2, (0,))
+    (held,) = local_call(functools.partial(choose_body, 0), [block], prev1, prev3_odd)
+    prev2 = swap(held)
+
+    pulled, *sent = local_call(
+        queries_body, [block32] + [square] * 3,
+        held_p, next1, next2, next3_even, next3_odd, weights[None, :], *coefs, token,
+        scratch=[pltpu.VMEM((rows, 5 * rows), BF16)],
+    )
+    came = [coefs[0]] + [shift(sent[n - 1], n) for n in range(1, 4)]
+    (base,) = local_call(
+        passages_body, [block32],
+        held_q, prev1, prev2, prev3_odd, weights[None, :], *came,
     )
     grad_queries, grad_passages = local_call(
-        functools.partial(finish_body, groups), [block, block], pulled, base, own1, *backs,
+        functools.partial(finish_body, groups), [block, block],
+        pulled, base, prev3_even, came[3], backs,
         out_specs=[HBM, HBM],
         scratch=[
             pltpu.VMEM((rows, width), BF16),

time: 87.3 us -> 97.5 us (1.12)
  waiting for transfers between devices: 45.7 us -> 37 us
  local copies, waits for them, and re-layouts: 3.14 us -> 11 us
  starting transfers between devices: 27.4 us -> 33.4 us
  Pallas kernels: 9.96 us -> 14.5 us
    ppermute x6 -> x9, waiting for transfers between devices: 36.5 us -> 28.1 us  [shift(): return lax.ppermute(array, 'blk', pairs)]
    unnamed x8 -> x38, local copies, waits for them, and re-layouts: 3.14 us -> 11 us
    pallas_call x13 -> x14, Pallas kernels: 9.96 us -> 14.5 us  [local_call(): pl.pallas_call(body, out_shape=out_shape, in_specs=in_specs or [VMEM] * l...]
    all_to_all x0 -> x1, starting transfers between devices: none -> 4.45 us  [per_device(): lax.all_to_all(backs, 'grp', split_axis=0, concat_axis=0, tiled=True)]
    ppermute x12 -> x9, starting transfers between devices: 14.2 us -> 10.6 us  [exchange(): out[r] = lax.ppermute(arrays[r], 'grp', [(i, i ^ r) for i in range(groups)])]
    ppermute x6 -> x9, starting transfers between devices: 12.3 us -> 15.1 us  [shift(): return lax.ppermute(array, 'blk', pairs)]
    ppermute x2, starting transfers between devices: 0.84 us -> 3.25 us  [swap(): return lax.ppermute(array, 'blk', [(i, i ^ 1) for i in range(loop)])]
    ppermute x12 -> x9, waiting for transfers between devices: 9.13 us -> 8.96 us  [exchange(): out[r] = lax.ppermute(arrays[r], 'grp', [(i, i ^ r) for i in range(groups)])]
  transfers between devices with their start and end apart: 20 -> 21, of which waited for: 10 -> 12; matrix products, arithmetic and copies ran while one was open for 0% -> 0% of each run, Pallas kernels for 8% -> 12%
where the time goes in v1:
time: 97.5 us; the launch traced here: 96.9 us
  waiting for transfers between devices  37 us (38%)
  starting transfers between devices  33.4 us (34%)
  Pallas kernels  14.5 us (15%)
  local copies, waits for them, and re-layouts  11 us (11%)
    ppermute x9, waiting for transfers between devices, shift(): return lax.ppermute(array, 'blk', pairs)  28.1 us
    ppermute x9, starting transfers between devices, shift(): return lax.ppermute(array, 'blk', pairs)  15.1 us
    pallas_call x14, Pallas kernels, local_call(): pl.pallas_call(body, out_shape=out_shape, in_specs=in_specs or [VMEM] * l...  14.5 us
    unnamed x38, local copies, waits for them, and re-layouts  11 us
    ppermute x9, starting transfers between devices, exchange(): out[r] = lax.ppermute(arrays[r], 'grp', [(i, i ^ r) for i in range(groups)])  10.6 us
    ppermute x9, waiting for transfers between devices, exchange(): out[r] = lax.ppermute(arrays[r], 'grp', [(i, i ^ r) for i in range(groups)])  8.96 us
    all_to_all x1, starting transfers between devices, per_device(): lax.all_to_all(backs, 'grp', split_axis=0, concat_axis=0, tiled=True)  4.45 us
    ppermute x2, starting transfers between devices, swap(): return lax.ppermute(array, 'blk', [(i, i ^ 1) for i in range(loop)])  3.25 us
  transfers between devices with their start and end apart: 21, of which 12 were waited for; matrix products, arithmetic and copies ran while one was open for 0% of the time, Pallas kernels for 12%

profile of v1, /device:TPU:0, one launch (start us, length us, event | category | flops | bytes accessed | tf_op | source)
XLA Modules:
  0.0 96.9 jit_solution(3476619500253320426)
XLA Ops:
  0.6 4.5 %collective-permute-start = (bf16[128,4096]{1,0:T(8,128)(2,1)}, bf16[128,4096]{1,0:T(8,128)(2,1)S(1)}, u32[]{:S(2)}, u32[]{:S(2)}) collective-permute-start(bf16[128,4096]{1,0:T(8,128)(2,1)} %p_hbm.1), channel_id=1, source_target_pairs={{0,7},{1,0},{2,1},{3,2},{4,3},{5,4},{6,5},{7,6},{8,15},{9,8},{10,9... | collective-permute-start | bytes 3145736 | tf_op jit(solution)/shard_map/ppermute | solution.py:238
  5.2 1.2 %copy-done.15 = bf16[128,4096]{1,0:T(8,128)(2,1)S(1)} copy-done((bf16[128,4096]{1,0:T(8,128)(2,1)S(1)}, bf16[128,4096]{1,0:T(8,128)(2,1)}, u32[]{:S(2)}) %copy-start.15) | copy-done | bytes 1048600
  6.4 1.2 %copy-done.16 = bf16[128,4096]{1,0:T(8,128)(2,1)S(1)} copy-done((bf16[128,4096]{1,0:T(8,128)(2,1)S(1)}, bf16[128,4096]{1,0:T(8,128)(2,1)}, u32[]{:S(2)}) %copy-start.16) | copy-done | bytes 1048600
  8.7 1.6 %collective-permute-start.4 = (bf16[272,1024]{1,0:T(8,128)(2,1)S(1)}, bf16[272,1024]{1,0:T(8,128)(2,1)S(1)}, u32[]{:S(2)}, u32[]{:S(2)}) collective-permute-start(bf16[272,1024]{1,0:T(8,128)(2,1)S(1)} %get-tuple-element.39), channel_id=1, source_target_pairs={{0,8},{8,0},{16,24},{24,16},{1,9},{9,1},{17,25},{25,17},{2,10},{10... | collective-permute-start | bytes 1671176 | tf_op jit(solution)/shard_map/ppermute | solution.py:246
  10.3 1.5 %collective-permute-start.5 = (bf16[272,1024]{1,0:T(8,128)(2,1)S(1)}, bf16[272,1024]{1,0:T(8,128)(2,1)S(1)}, u32[]{:S(2)}, u32[]{:S(2)}) collective-permute-start(bf16[272,1024]{1,0:T(8,128)(2,1)S(1)} %get-tuple-element.40), channel_id=1, source_target_pairs={{0,16},{8,24},{16,0},{24,8},{1,17},{9,25},{17,1},{25,9},{2,18},{10... | collective-permute-start | bytes 1671176 | tf_op jit(solution)/shard_map/ppermute | solution.py:246
  12.3 1.3 %collective-permute-start.1 = (bf16[128,4096]{1,0:T(8,128)(2,1)S(1)}, bf16[128,4096]{1,0:T(8,128)(2,1)S(1)}, u32[]{:S(2)}, u32[]{:S(2)}) collective-permute-start(bf16[128,4096]{1,0:T(8,128)(2,1)S(1)} %get-tuple-element.33.refs_0_.p_ref), channel_id=1, source_target_pairs={{1,6},{3,0},{5,2},{7,4},{9,14},{11,8},{13,10},{15,12},{17,22},{19,... | collective-permute-start | bytes 3145736 | tf_op jit(solution)/shard_map/ppermute | solution.py:238
  13.5 6.7 %collective-permute-done.source = bf16[128,4096]{1,0:T(8,128)(2,1)S(1)} collective-permute-done((bf16[128,4096]{1,0:T(8,128)(2,1)}, bf16[128,4096]{1,0:T(8,128)(2,1)S(1)}, u32[]{:S(2)}, u32[]{:S(2)}) %collective-permute-start) | collective-permute-done | bytes 1048608 | tf_op jit(solution)/shard_map/ppermute | solution.py:238
  21.0 7.3 %collective-permute-done.1.refs_2_.second_ref.e3_ref = bf16[128,4096]{1,0:T(8,128)(2,1)S(1)} collective-permute-done((bf16[128,4096]{1,0:T(8,128)(2,1)S(1)}, bf16[128,4096]{1,0:T(8,128)(2,1)S(1)}, u32[]{:S(2)}, u32[]{:S(2)}) %collective-permute-start.1) | collective-permute-done | bytes 1048608 | tf_op jit(solution)/shard_map/ppermute | solution.py:238
  30.3 3.6 %collective-permute-done.5.refs_2_ = bf16[272,1024]{1,0:T(8,128)(2,1)S(1)} collective-permute-done((bf16[272,1024]{1,0:T(8,128)(2,1)S(1)}, bf16[272,1024]{1,0:T(8,128)(2,1)S(1)}, u32[]{:S(2)}, u32[]{:S(2)}) %collective-permute-start.5) | collective-permute-done | bytes 557088 | tf_op jit(solution)/shard_map/ppermute | solution.py:246
  33.9 2.4 %shard_map.72 = (f32[3,128]{1,0:T(4,128)S(1)}, f32[3,128]{1,0:T(4,128)S(1)}, f32[3,128]{1,0:T(4,128)S(1)}, f32[3,128]{1,0:T(4,128)S(1)}, bf16[128,4096]{1,0:T(8,128)(2,1)}) custom-call(bf16[128,4096]{1,0:T(8,128)(2,1)S(1)} %get-tuple-element.32.q_ref.source, bf16[272,1024]{1,0:T(8,128)(2,1)S(1)} %get-tuple-element.38.refs_0_, ...), custom_call_target="tpu_custom_call" | custom-call | flops 49999998976 | bytes 4397056 | tf_op jit(solution)/shard_map/pallas_call | solution.py:31
  36.3 1.2 %collective-permute-start.7 = (f32[3,128]{1,0:T(4,128)S(1)}, f32[3,128]{1,0:T(4,128)S(1)}, u32[]{:S(2)}, u32[]{:S(2)}) collective-permute-start(f32[3,128]{1,0:T(4,128)S(1)} %get-tuple-element.43), channel_id=1, source_target_pairs={{0,8},{8,0},{16,24},{24,16},{1,9},{9,1},{17,25},{25,17},{2,10},{10... | collective-permute-start | bytes 4616 | tf_op jit(solution)/shard_map/ppermute | solution.py:246
  38.3 1.4 %collective-permute-start.9 = (f32[3,128]{1,0:T(4,128)S(1)}, f32[3,128]{1,0:T(4,128)S(1)}, u32[]{:S(2)}, u32[]{:S(2)}) collective-permute-start(f32[3,128]{1,0:T(4,128)S(1)} %get-tuple-element.45), channel_id=1, source_target_pairs={{0,24},{8,16},{16,8},{24,0},{1,25},{9,17},{17,9},{25,1},{2,26},{10... | collective-permute-start | bytes 4616 | tf_op jit(solution)/shard_map/ppermute | solution.py:246
  41.1 1.7 %collective-permute-done.9.refs_3_ = f32[3,128]{1,0:T(4,128)S(1)} collective-permute-done((f32[3,128]{1,0:T(4,128)S(1)}, f32[3,128]{1,0:T(4,128)S(1)}, u32[]{:S(2)}, u32[]{:S(2)}) %collective-permute-start.9) | collective-permute-done | bytes 1568 | tf_op jit(solution)/shard_map/ppermute | solution.py:246
  44.9 2.3 %collective-permute-start.14 = (bf16[128,4096]{1,0:T(8,128)(2,1)}, bf16[128,4096]{1,0:T(8,128)(2,1)S(1)}, u32[]{:S(2)}, u32[]{:S(2)}) collective-permute-start(bf16[128,4096]{1,0:T(8,128)(2,1)} %shard_map.77), channel_id=1, source_target_pairs={{0,3},{2,5},{4,7},{6,1},{8,11},{10,13},{12,15},{14,9},{16,19},{18,... | collective-permute-start | bytes 3145736 | tf_op jit(solution)/shard_map/ppermute | solution.py:238
  47.2 1.6 %collective-permute-start.12 = (f32[3,128]{1,0:T(4,128)S(1)}, f32[3,128]{1,0:T(4,128)S(1)}, u32[]{:S(2)}, u32[]{:S(2)}) collective-permute-start(f32[3,128]{1,0:T(4,128)S(1)} %get-tuple-element.51.refs_4_.token), channel_id=1, source_target_pairs={{0,24},{8,16},{16,8},{24,0},{1,25},{9,17},{17,9},{25,1},{2,26},{10... | collective-permute-start | bytes 4616 | tf_op jit(solution)/shard_map/ppermute | solution.py:246
  48.8 1.2 %collective-permute-start.11 = (f32[3,128]{1,0:T(4,128)S(1)}, f32[3,128]{1,0:T(4,128)S(1)}, u32[]{:S(2)}, u32[]{:S(2)}) collective-permute-start(f32[3,128]{1,0:T(4,128)S(1)} %get-tuple-element.51.refs_4_.token), channel_id=1, source_target_pairs={{0,16},{8,24},{16,0},{24,8},{1,17},{9,25},{17,1},{25,9},{2,18},{10... | collective-permute-start | bytes 4616 | tf_op jit(solution)/shard_map/ppermute | solution.py:246
  52.4 1.2 %collective-permute-done.10.refs_5_ = f32[3,128]{1,0:T(4,128)S(1)} collective-permute-done((f32[3,128]{1,0:T(4,128)S(1)}, f32[3,128]{1,0:T(4,128)S(1)}, u32[]{:S(2)}, u32[]{:S(2)}) %collective-permute-start.10) | collective-permute-done | bytes 1568 | tf_op jit(solution)/shard_map/ppermute | solution.py:246
  53.6 1.6 %shard_map.74 = (bf16[4,256,1024]{2,1,0:T(8,128)(2,1)S(1)}, f32[8,128]{1,0:T(8,128)S(1)}) custom-call(bf16[272,1024]{1,0:T(8,128)(2,1)S(1)} %get-tuple-element.38.refs_0_, bf16[272,1024]{1,0:T(8,128)(2,1)S(1)} %collective-permute-done.4.refs_1_, bf16[272,1024]{1,0:T(8,128)(2,1)S(1)} %collective-permute-done.5.refs_2_, ...), custom_call_target="tpu_custom_call" | custom-call | bytes 4335616 | tf_op jit(solution)/shard_map/pallas_call | solution.py:31
  55.2 1.3 %copy-done.12 = bf16[4,256,1024]{2,1,0:T(8,128)(2,1)} copy-done((bf16[4,256,1024]{2,1,0:T(8,128)(2,1)}, bf16[4,256,1024]{2,1,0:T(8,128)(2,1)S(1)}, u32[]{:S(2)}) %copy-start.12) | copy-done | bytes 2097176
  56.5 4.4 %all-to-all-start = ((bf16[4,256,1024]{2,1,0:T(8,128)(2,1)}), bf16[4,256,1024]{2,1,0:T(8,128)(2,1)}, u32[]{:S(2)}, u32[]{:S(2)}) async-start(bf16[4,256,1024]{2,1,0:T(8,128)(2,1)} %copy-done.12), calls=%async_computation | async-start | bytes 4194304 | tf_op jit(solution)/shard_map/all_to_all | solution.py:297
  61.0 1.4 %shard_map.76.first_ref.m1_ref = bf16[128,4096]{1,0:T(8,128)(2,1)S(1)} custom-call(bf16[128,4096]{1,0:T(8,128)(2,1)} %collective-permute-done.13.source, f32[8,128]{1,0:T(8,128)S(1)} %get-tuple-element.52.refs_4_.token), custom_call_target="tpu_custom_call" | custom-call | bytes 2101248 | tf_op jit(solution)/shard_map/pallas_call | solution.py:31
  62.4 2.3 %collective-permute-done.14.second_ref.u3_ref = bf16[128,4096]{1,0:T(8,128)(2,1)S(1)} collective-permute-done((bf16[128,4096]{1,0:T(8,128)(2,1)}, bf16[128,4096]{1,0:T(8,128)(2,1)S(1)}, u32[]{:S(2)}, u32[]{:S(2)}) %collective-permute-start.14) | collective-permute-done | bytes 1048608 | tf_op jit(solution)/shard_map/ppermute | solution.py:238
  64.7 2.5 %collective-permute-start.15 = (bf16[128,4096]{1,0:T(8,128)(2,1)S(1)}, bf16[128,4096]{1,0:T(8,128)(2,1)S(1)}, u32[]{:S(2)}, u32[]{:S(2)}) collective-permute-start(bf16[128,4096]{1,0:T(8,128)(2,1)S(1)} %shard_map.78), channel_id=1, source_target_pairs={{0,1},{1,0},{2,3},{3,2},{4,5},{5,4},{6,7},{7,6},{8,9},{9,8},{10,11... | collective-permute-start | bytes 3145736 | tf_op jit(solution)/shard_map/ppermute | solution.py:241
  67.2 1.9 %collective-permute-start.19 = (bf16[128,4096]{1,0:T(8,128)(2,1)S(1)}, bf16[128,4096]{1,0:T(8,128)(2,1)S(1)}, u32[]{:S(2)}, u32[]{:S(2)}) collective-permute-start(bf16[128,4096]{1,0:T(8,128)(2,1)S(1)} %shard_map.76.first_ref.m1_ref), channel_id=1, source_target_pairs={{0,2},{2,4},{4,6},{6,0},{8,10},{10,12},{12,14},{14,8},{16,18},{18,... | collective-permute-start | bytes 3145736 | tf_op jit(solution)/shard_map/ppermute | solution.py:238
  70.3 1.4 %copy-done.10 = f32[128,4096]{1,0:T(8,128)} copy-done((f32[128,4096]{1,0:T(8,128)}, f32[128,4096]{1,0:T(8,128)S(1)}, u32[]{:S(2)}) %copy-start.10) | copy-done | bytes 2097176
  71.6 1.8 %collective-permute-start.17 = (bf16[128,128]{1,0:T(8,128)(2,1)S(1)}, bf16[128,128]{1,0:T(8,128)(2,1)S(1)}, u32[]{:S(2)}, u32[]{:S(2)}) collective-permute-start(bf16[128,128]{1,0:T(8,128)(2,1)S(1)} %get-tuple-element.56), channel_id=1, source_target_pairs={{0,2},{1,3},{2,4},{3,5},{4,6},{5,7},{6,0},{7,1},{8,10},{9,11},{10,... | collective-permute-start | bytes 98312 | tf_op jit(solution)/shard_map/ppermute | solution.py:238
  73.4 2.6 %collective-permute-start.18 = (bf16[128,128]{1,0:T(8,128)(2,1)S(1)}, bf16[128,128]{1,0:T(8,128)(2,1)S(1)}, u32[]{:S(2)}, u32[]{:S(2)}) collective-permute-start(bf16[128,128]{1,0:T(8,128)(2,1)S(1)} %get-tuple-element.57), channel_id=1, source_target_pairs={{0,3},{1,4},{2,5},{3,6},{4,7},{5,0},{6,1},{7,2},{8,11},{9,12},{10,... | collective-permute-start | bytes 98312 | tf_op jit(solution)/shard_map/ppermute | solution.py:238
  77.2 10.0 %collective-permute-done.17.refs_2_ = bf16[128,128]{1,0:T(8,128)(2,1)S(1)} collective-permute-done((bf16[128,128]{1,0:T(8,128)(2,1)S(1)}, bf16[128,128]{1,0:T(8,128)(2,1)S(1)}, u32[]{:S(2)}, u32[]{:S(2)}) %collective-permute-start.17) | collective-permute-done | bytes 32800 | tf_op jit(solution)/shard_map/ppermute | solution.py:238
  87.8 1.2 %copy-done.1 = bf16[128,4096]{1,0:T(8,128)(2,1)S(1)} copy-done((bf16[128,4096]{1,0:T(8,128)(2,1)S(1)}, bf16[128,4096]{1,0:T(8,128)(2,1)}, u32[]{:S(2)}) %copy-start.1) | copy-done | bytes 1048600
  90.8 1.6 %copy-done.11 = f32[128,4096]{1,0:T(8,128)S(1)} copy-done((f32[128,4096]{1,0:T(8,128)S(1)}, f32[128,4096]{1,0:T(8,128)}, u32[]{:S(2)}) %copy-start.11) | copy-done | bytes 2097176
  92.3 1.2 %copy-done.14 = bf16[128,4096]{1,0:T(8,128)(2,1)S(1)} copy-done((bf16[128,4096]{1,0:T(8,128)(2,1)S(1)}, bf16[128,4096]{1,0:T(8,128)(2,1)}, u32[]{:S(2)}) %copy-start.14) | copy-done | bytes 1048600
  93.6 3.3 %shard_map.80 = (bf16[128,4096]{1,0:T(8,128)(2,1)}, bf16[128,4096]{1,0:T(8,128)(2,1)}) custom-call(f32[128,4096]{1,0:T(8,128)S(1)} %copy-done.11, f32[128,4096]{1,0:T(8,128)S(1)} %shard_map.79.base, bf16[128,4096]{1,0:T(8,128)(2,1)S(1)} %copy-done.14, bf16[128,128]{1,0:T(8,128)(2,1)S(1)} %collective-permute-done.18.refs_3_.coef3, ...), custom_call_target="tpu_custom_call" | custom-call | bytes 9469952 | tf_op jit(solution)/shard_map/pallas_call | solution.py:31
  (62 shorter events, 15.6 us)
Async XLA Ops:
  0.6 19.6 %collective-permute-start = (bf16[128,4096]{1,0:T(8,128)(2,1)}, bf16[128,4096]{1,0:T(8,128)(2,1)S(1)}, u32[]{:S(2)}, u32[]{:S(2)}) collective-permute-start(bf16[128,4096]{1,0:T(8,128)(2,1)} %p_hbm.1), channel_id=1, source_target_pairs={{0,7},{1,0},{2,1},{3,2},{4,3},{5,4},{6,5},{7,6},{8,15},{9,8},{10,9... | collective-permute-start | bytes 3145736 | tf_op jit(solution)/shard_map/ppermute | solution.py:238
  8.7 20.5 %copy-start.4 = (bf16[128,4096]{1,0:T(8,128)(2,1)}, bf16[128,4096]{1,0:T(8,128)(2,1)S(1)}, u32[]{:S(2)}) copy-start(bf16[128,4096]{1,0:T(8,128)(2,1)S(1)} %get-tuple-element.33.refs_0_.p_ref) | copy-start | bytes 3145732
  8.7 21.6 %collective-permute-start.4 = (bf16[272,1024]{1,0:T(8,128)(2,1)S(1)}, bf16[272,1024]{1,0:T(8,128)(2,1)S(1)}, u32[]{:S(2)}, u32[]{:S(2)}) collective-permute-start(bf16[272,1024]{1,0:T(8,128)(2,1)S(1)} %get-tuple-element.39), channel_id=1, source_target_pairs={{0,8},{8,0},{16,24},{24,16},{1,9},{9,1},{17,25},{25,17},{2,10},{10... | collective-permute-start | bytes 1671176 | tf_op jit(solution)/shard_map/ppermute | solution.py:246
  10.3 23.7 %collective-permute-start.5 = (bf16[272,1024]{1,0:T(8,128)(2,1)S(1)}, bf16[272,1024]{1,0:T(8,128)(2,1)S(1)}, u32[]{:S(2)}, u32[]{:S(2)}) collective-permute-start(bf16[272,1024]{1,0:T(8,128)(2,1)S(1)} %get-tuple-element.40), channel_id=1, source_target_pairs={{0,16},{8,24},{16,0},{24,8},{1,17},{9,25},{17,1},{25,9},{2,18},{10... | collective-permute-start | bytes 1671176 | tf_op jit(solution)/shard_map/ppermute | solution.py:246
  11.8 22.1 %collective-permute-start.6 = (bf16[272,1024]{1,0:T(8,128)(2,1)S(1)}, bf16[272,1024]{1,0:T(8,128)(2,1)S(1)}, u32[]{:S(2)}, u32[]{:S(2)}) collective-permute-start(bf16[272,1024]{1,0:T(8,128)(2,1)S(1)} %get-tuple-element.41), channel_id=1, source_target_pairs={{0,24},{8,16},{16,8},{24,0},{1,25},{9,17},{17,9},{25,1},{2,26},{10... | collective-permute-start | bytes 1671176 | tf_op jit(solution)/shard_map/ppermute | solution.py:246
  12.3 16.1 %collective-permute-start.1 = (bf16[128,4096]{1,0:T(8,128)(2,1)S(1)}, bf16[128,4096]{1,0:T(8,128)(2,1)S(1)}, u32[]{:S(2)}, u32[]{:S(2)}) collective-permute-start(bf16[128,4096]{1,0:T(8,128)(2,1)S(1)} %get-tuple-element.33.refs_0_.p_ref), channel_id=1, source_target_pairs={{1,6},{3,0},{5,2},{7,4},{9,14},{11,8},{13,10},{15,12},{17,22},{19,... | collective-permute-start | bytes 3145736 | tf_op jit(solution)/shard_map/ppermute | solution.py:238
  20.3 8.9 %copy-start.8 = (bf16[128,4096]{1,0:T(8,128)(2,1)}, bf16[128,4096]{1,0:T(8,128)(2,1)S(1)}, u32[]{:S(2)}) copy-start(bf16[128,4096]{1,0:T(8,128)(2,1)S(1)} %shard_map.68.refs_1_.first_ref.n1_ref) | copy-start | bytes 3145732
  20.3 22.5 %collective-permute-start.3 = (bf16[128,4096]{1,0:T(8,128)(2,1)S(1)}, bf16[128,4096]{1,0:T(8,128)(2,1)S(1)}, u32[]{:S(2)}, u32[]{:S(2)}) collective-permute-start(bf16[128,4096]{1,0:T(8,128)(2,1)S(1)} %shard_map.68.refs_1_.first_ref.n1_ref), channel_id=1, source_target_pairs={{1,7},{3,1},{5,3},{7,5},{9,15},{11,9},{13,11},{15,13},{17,23},{19,... | collective-permute-start | bytes 3145736 | tf_op jit(solution)/shard_map/ppermute | solution.py:238
  28.4 11.3 %collective-permute-start.2 = (bf16[128,4096]{1,0:T(8,128)(2,1)S(1)}, bf16[128,4096]{1,0:T(8,128)(2,1)S(1)}, u32[]{:S(2)}, u32[]{:S(2)}) collective-permute-start(bf16[128,4096]{1,0:T(8,128)(2,1)S(1)} %shard_map.70), channel_id=1, source_target_pairs={{0,1},{1,0},{2,3},{3,2},{4,5},{5,4},{6,7},{7,6},{8,9},{9,8},{10,11... | collective-permute-start | bytes 3145736 | tf_op jit(solution)/shard_map/ppermute | solution.py:241
  36.3 6.5 %copy-start.17 = (f32[128]{0:T(128)S(1)}, f32[128]{0:T(128)}, u32[]{:S(2)}) copy-start(f32[128]{0:T(128)} %param.7) | copy-start | bytes 1540
  36.3 3.9 %collective-permute-start.7 = (f32[3,128]{1,0:T(4,128)S(1)}, f32[3,128]{1,0:T(4,128)S(1)}, u32[]{:S(2)}, u32[]{:S(2)}) collective-permute-start(f32[3,128]{1,0:T(4,128)S(1)} %get-tuple-element.43), channel_id=1, source_target_pairs={{0,8},{8,0},{16,24},{24,16},{1,9},{9,1},{17,25},{25,17},{2,10},{10... | collective-permute-start | bytes 4616 | tf_op jit(solution)/shard_map/ppermute | solution.py:246
  37.5 3.6 %collective-permute-start.8 = (f32[3,128]{1,0:T(4,128)S(1)}, f32[3,128]{1,0:T(4,128)S(1)}, u32[]{:S(2)}, u32[]{:S(2)}) collective-permute-start(f32[3,128]{1,0:T(4,128)S(1)} %get-tuple-element.44), channel_id=1, source_target_pairs={{0,16},{8,24},{16,0},{24,8},{1,17},{9,25},{17,1},{25,9},{2,18},{10... | collective-permute-start | bytes 4616 | tf_op jit(solution)/shard_map/ppermute | solution.py:246
  38.3 4.5 %collective-permute-start.9 = (f32[3,128]{1,0:T(4,128)S(1)}, f32[3,128]{1,0:T(4,128)S(1)}, u32[]{:S(2)}, u32[]{:S(2)}) collective-permute-start(f32[3,128]{1,0:T(4,128)S(1)} %get-tuple-element.45), channel_id=1, source_target_pairs={{0,24},{8,16},{16,8},{24,0},{1,25},{9,17},{17,9},{25,1},{2,26},{10... | collective-permute-start | bytes 4616 | tf_op jit(solution)/shard_map/ppermute | solution.py:246
  39.8 21.2 %collective-permute-start.13 = (bf16[128,4096]{1,0:T(8,128)(2,1)}, bf16[128,4096]{1,0:T(8,128)(2,1)}, u32[]{:S(2)}, u32[]{:S(2)}) collective-permute-start(bf16[128,4096]{1,0:T(8,128)(2,1)} %get-tuple-element.54), channel_id=1, source_target_pairs={{0,1},{1,2},{2,3},{3,4},{4,5},{5,6},{6,7},{7,0},{8,9},{9,10},{10,1... | collective-permute-start | bytes 3145736 | tf_op jit(solution)/shard_map/ppermute | solution.py:238
  44.9 19.7 %collective-permute-start.14 = (bf16[128,4096]{1,0:T(8,128)(2,1)}, bf16[128,4096]{1,0:T(8,128)(2,1)S(1)}, u32[]{:S(2)}, u32[]{:S(2)}) collective-permute-start(bf16[128,4096]{1,0:T(8,128)(2,1)} %shard_map.77), channel_id=1, source_target_pairs={{0,3},{2,5},{4,7},{6,1},{8,11},{10,13},{12,15},{14,9},{16,19},{18,... | collective-permute-start | bytes 3145736 | tf_op jit(solution)/shard_map/ppermute | solution.py:238
  47.2 4.5 %collective-permute-start.12 = (f32[3,128]{1,0:T(4,128)S(1)}, f32[3,128]{1,0:T(4,128)S(1)}, u32[]{:S(2)}, u32[]{:S(2)}) collective-permute-start(f32[3,128]{1,0:T(4,128)S(1)} %get-tuple-element.51.refs_4_.token), channel_id=1, source_target_pairs={{0,24},{8,16},{16,8},{24,0},{1,25},{9,17},{17,9},{25,1},{2,26},{10... | collective-permute-start | bytes 4616 | tf_op jit(solution)/shard_map/ppermute | solution.py:246
  48.8 3.6 %collective-permute-start.11 = (f32[3,128]{1,0:T(4,128)S(1)}, f32[3,128]{1,0:T(4,128)S(1)}, u32[]{:S(2)}, u32[]{:S(2)}) collective-permute-start(f32[3,128]{1,0:T(4,128)S(1)} %get-tuple-element.51.refs_4_.token), channel_id=1, source_target_pairs={{0,16},{8,24},{16,0},{24,8},{1,17},{9,25},{17,1},{25,9},{2,18},{10... | collective-permute-start | bytes 4616 | tf_op jit(solution)/shard_map/ppermute | solution.py:246
  50.0 3.6 %collective-permute-start.10 = (f32[3,128]{1,0:T(4,128)S(1)}, f32[3,128]{1,0:T(4,128)S(1)}, u32[]{:S(2)}, u32[]{:S(2)}) collective-permute-start(f32[3,128]{1,0:T(4,128)S(1)} %get-tuple-element.51.refs_4_.token), channel_id=1, source_target_pairs={{0,8},{8,0},{16,24},{24,16},{1,9},{9,1},{17,25},{25,17},{2,10},{10... | collective-permute-start | bytes 4616 | tf_op jit(solution)/shard_map/ppermute | solution.py:246
  55.1 1.3 %copy-start.12 = (bf16[4,256,1024]{2,1,0:T(8,128)(2,1)}, bf16[4,256,1024]{2,1,0:T(8,128)(2,1)S(1)}, u32[]{:S(2)}) copy-start(bf16[4,256,1024]{2,1,0:T(8,128)(2,1)S(1)} %get-tuple-element.58) | copy-start | bytes 6291460
  56.5 34.3 %all-to-all-start = ((bf16[4,256,1024]{2,1,0:T(8,128)(2,1)}), bf16[4,256,1024]{2,1,0:T(8,128)(2,1)}, u32[]{:S(2)}, u32[]{:S(2)}) async-start(bf16[4,256,1024]{2,1,0:T(8,128)(2,1)} %copy-done.12), calls=%async_computation | async-start | bytes 4194304 | tf_op jit(solution)/shard_map/all_to_all | solution.py:297
  61.0 8.2 %copy-start.9 = (bf16[128,4096]{1,0:T(8,128)(2,1)S(1)}, bf16[128,4096]{1,0:T(8,128)(2,1)}, u32[]{:S(2)}) copy-start(bf16[128,4096]{1,0:T(8,128)(2,1)} %copy-done.8) | copy-start | bytes 3145732
  62.4 6.8 %copy-start.3 = (bf16[128,4096]{1,0:T(8,128)(2,1)S(1)}, bf16[128,4096]{1,0:T(8,128)(2,1)}, u32[]{:S(2)}) copy-start(bf16[128,4096]{1,0:T(8,128)(2,1)} %copy-done.2) | copy-start | bytes 3145732
  62.4 6.8 %copy-start.5 = (bf16[128,4096]{1,0:T(8,128)(2,1)S(1)}, bf16[128,4096]{1,0:T(8,128)(2,1)}, u32[]{:S(2)}) copy-start(bf16[128,4096]{1,0:T(8,128)(2,1)} %copy-done.4) | copy-start | bytes 3145732
  62.4 6.8 %copy-start.7 = (bf16[128,4096]{1,0:T(8,128)(2,1)S(1)}, bf16[128,4096]{1,0:T(8,128)(2,1)}, u32[]{:S(2)}) copy-start(bf16[128,4096]{1,0:T(8,128)(2,1)} %copy-done.6) | copy-start | bytes 3145732
  64.6 5.6 %copy-start = (bf16[128,4096]{1,0:T(8,128)(2,1)}, bf16[128,4096]{1,0:T(8,128)(2,1)S(1)}, u32[]{:S(2)}) copy-start(bf16[128,4096]{1,0:T(8,128)(2,1)S(1)} %collective-permute-done.14.second_ref.u3_ref) | copy-start | bytes 3145732
  64.7 23.1 %collective-permute-start.15 = (bf16[128,4096]{1,0:T(8,128)(2,1)S(1)}, bf16[128,4096]{1,0:T(8,128)(2,1)S(1)}, u32[]{:S(2)}, u32[]{:S(2)}) collective-permute-start(bf16[128,4096]{1,0:T(8,128)(2,1)S(1)} %shard_map.78), channel_id=1, source_target_pairs={{0,1},{1,0},{2,3},{3,2},{4,5},{5,4},{6,7},{7,6},{8,9},{9,8},{10,11... | collective-permute-start | bytes 3145736 | tf_op jit(solution)/shard_map/ppermute | solution.py:241
  67.2 22.6 %collective-permute-start.19 = (bf16[128,4096]{1,0:T(8,128)(2,1)S(1)}, bf16[128,4096]{1,0:T(8,128)(2,1)S(1)}, u32[]{:S(2)}, u32[]{:S(2)}) collective-permute-start(bf16[128,4096]{1,0:T(8,128)(2,1)S(1)} %shard_map.76.first_ref.m1_ref), channel_id=1, source_target_pairs={{0,2},{2,4},{4,6},{6,0},{8,10},{10,12},{12,14},{14,8},{16,18},{18,... | collective-permute-start | bytes 3145736 | tf_op jit(solution)/shard_map/ppermute | solution.py:238
  70.3 1.4 %copy-start.10 = (f32[128,4096]{1,0:T(8,128)}, f32[128,4096]{1,0:T(8,128)S(1)}, u32[]{:S(2)}) copy-start(f32[128,4096]{1,0:T(8,128)S(1)} %get-tuple-element.53.pulled) | copy-start | bytes 6291460
  71.6 5.6 %collective-permute-start.16 = (bf16[128,128]{1,0:T(8,128)(2,1)S(1)}, bf16[128,128]{1,0:T(8,128)(2,1)S(1)}, u32[]{:S(2)}, u32[]{:S(2)}) collective-permute-start(bf16[128,128]{1,0:T(8,128)(2,1)S(1)} %get-tuple-element.55), channel_id=1, source_target_pairs={{0,1},{1,2},{2,3},{3,4},{4,5},{5,6},{6,7},{7,0},{8,9},{9,10},{10,1... | collective-permute-start | bytes 98312 | tf_op jit(solution)/shard_map/ppermute | solution.py:238
  71.6 15.6 %collective-permute-start.17 = (bf16[128,128]{1,0:T(8,128)(2,1)S(1)}, bf16[128,128]{1,0:T(8,128)(2,1)S(1)}, u32[]{:S(2)}, u32[]{:S(2)}) collective-permute-start(bf16[128,128]{1,0:T(8,128)(2,1)S(1)} %get-tuple-element.56), channel_id=1, source_target_pairs={{0,2},{1,3},{2,4},{3,5},{4,6},{5,7},{6,0},{7,1},{8,10},{9,11},{10,... | collective-permute-start | bytes 98312 | tf_op jit(solution)/shard_map/ppermute | solution.py:238
  73.4 14.4 %collective-permute-start.18 = (bf16[128,128]{1,0:T(8,128)(2,1)S(1)}, bf16[128,128]{1,0:T(8,128)(2,1)S(1)}, u32[]{:S(2)}, u32[]{:S(2)}) collective-permute-start(bf16[128,128]{1,0:T(8,128)(2,1)S(1)} %get-tuple-element.57), channel_id=1, source_target_pairs={{0,3},{1,4},{2,5},{3,6},{4,7},{5,0},{6,1},{7,2},{8,11},{9,12},{10,... | collective-permute-start | bytes 98312 | tf_op jit(solution)/shard_map/ppermute | solution.py:238
  90.8 1.6 %copy-start.11 = (f32[128,4096]{1,0:T(8,128)S(1)}, f32[128,4096]{1,0:T(8,128)}, u32[]{:S(2)}) copy-start(f32[128,4096]{1,0:T(8,128)} %copy-done.10) | copy-start | bytes 6291460
  (8 other events, 8.6 us)

commit v2 on v0

--- a/solution.py
+++ b/solution.py
@@ -13,6 +13,7 @@
 F32 = jnp.float32
 CHUNK = 512
 TAIL = 16
+SLOT = 8
 LONG, SOME = 5 * 10**10, 16 * 10**9
 VMEM = pl.BlockSpec(memory_space=pltpu.VMEM)
 HBM = pl.BlockSpec(memory_space=pltpu.HBM)
@@ -87,23 +88,46 @@
     return [(tail[k : k + 1, :rows] ^ g) * rows + tail[k : k + 1, rows:] for k in range(3)]
 
 
+def bit_order(groups):
+    order = [0]
+    while len(order) < groups:
+        order = [2 * r for r in order] + [2 * r + 1 for r in order]
+    return order
+
+
 def hard_scores_body(groups, *refs):
-    pieces, outs = refs[:groups], refs[groups + 1 :]
-    rows = outs[0].shape[1]
+    pieces, (keep, give) = refs[:groups], refs[groups + 1 :]
+    rows = keep.shape[1]
     ids = lax.broadcasted_iota(jnp.int32, (groups * rows, rows), 0)
     p_all = jnp.concatenate([piece[rows : 2 * rows] for piece in pieces], axis=0)
-    for r in range(groups):
+    keep[...] = jnp.zeros(keep.shape, F32)
+    give[...] = jnp.zeros(give.shape, F32)
+    for n, r in enumerate(bit_order(groups)):
         places = places_of(pieces[r], rows)
         dots = dot(p_all, pieces[r][:rows], ((1,), (1,)))
+        out, slot = (keep, n) if n < groups // 2 else (give, n - groups // 2)
         for k in range(3):
             hit = jnp.where(ids == places[k], dots, 0.0)
-            outs[r][k : k + 1] = jnp.sum(hit, axis=0, keepdims=True)
+            at = SLOT * slot + k
+            out[at : at + 1] = jnp.sum(hit, axis=0, keepdims=True)
+
+
+def halve_body(mine_ref, came_ref, keep, give):
+    half = mine_ref.shape[0] // 2
+    keep[...] = mine_ref[:half] + came_ref[:half]
+    give[...] = mine_ref[half:] + came_ref[half:]
+
+
+def double_body(mine_ref, came_ref, out):
+    half = mine_ref.shape[0]
+    out[:half] = mine_ref[...]
+    out[half:] = came_ref[...]
 
 
 def hard_grads_body(groups, *refs):
-    pieces, coefs, outs = refs[:groups], refs[groups : 2 * groups], refs[2 * groups + 1 : 3 * groups + 1]
-    token, matrix, matrix_t = refs[3 * groups + 1 :]
-    rows = coefs[0].shape[1]
+    pieces, coefs, outs = refs[:groups], refs[groups], refs[groups + 2 : 2 * groups + 2]
+    token, matrix, matrix_t = refs[2 * groups + 2 :]
+    rows = coefs.shape[1]
     cols = outs[0].shape[1]
     signal(token)
     ids = lax.broadcasted_iota(jnp.int32, (groups * rows, rows), 0)
@@ -111,7 +135,7 @@
         places = places_of(pieces[r], rows)
         total = jnp.zeros(ids.shape, F32)
         for k in range(3):
-            total += jnp.where(ids == places[k], coefs[r][k : k + 1], 0.0)
+            total += jnp.where(ids == places[k], coefs[SLOT * r + k : SLOT * r + k + 1], 0.0)
         mine = slice(r * rows, (r + 1) * rows)
         matrix[:, mine] = total.astype(BF16)
         matrix_t[mine] = total.T.astype(BF16)
@@ -150,17 +174,15 @@
         out[...] = dot(block[...], q_ref[...], ((1,), (1,)))
 
 
-def weigh_body(groups, q_ref, s0_ref, s1_ref, s2_ref, s3_ref, last_ref, w_ref, *refs):
-    hard_refs = refs[:groups]
-    loss_ref, coef_ref, hard_out, term3_ref, term2_ref = refs[groups:]
+def weigh_body(
+    q_ref, s0_ref, s1_ref, s2_ref, s3_ref, last_ref, w_ref, hard_mine, hard_came, other_ref,
+    loss_ref, coef_ref, hard_out, swap_ref, term3_ref,
+):
     rows, width = q_ref.shape
     w = w_ref[...]
     s3 = INV_TEMP * (s3_ref[...] + dot(last_ref[...], q_ref[...], ((1,), (1,))))
     scores = [INV_TEMP * s0_ref[...], INV_TEMP * s1_ref[...], INV_TEMP * s2_ref[...], s3]
-    hard = hard_refs[0][...]
-    for other in hard_refs[1:]:
-        hard = hard + other[...]
-    hard = INV_TEMP * hard
+    hard = INV_TEMP * (hard_mine[:3] + hard_came[:3])
     largest = jnp.max(hard, axis=0, keepdims=True)
     for block in scores:
         largest = jnp.maximum(largest, jnp.max(block, axis=0, keepdims=True))
@@ -168,32 +190,35 @@
     for block in scores:
         summed = summed + jnp.sum(jnp.exp(block - largest), axis=0, keepdims=True)
     log_total = largest + jnp.log(summed)
-    for s in range(4):
-        coef_ref[s * rows : (s + 1) * rows] = (w * jnp.exp(scores[s] - log_total)).astype(BF16)
+    for s, block in enumerate(scores):
+        coef = (w * jnp.exp(block - log_total)).astype(BF16)
+        coef_ref[:, s * rows : (s + 1) * rows] = coef
+        if s in (1, 2):
+            swap_ref[:, (s - 1) * rows : s * rows] = coef
+    coef3 = coef_ref[:, 3 * rows :]
     for c in range(0, width, CHUNK):
         at = slice(c, c + CHUNK)
-        both = dot(coef_ref[2 * rows :], q_ref[:, at], ((1,), (0,))).astype(BF16)
-        term2_ref[:, at] = both[:rows]
-        term3_ref[:, at] = both[rows:]
-    hard_out[...] = (w * jnp.exp(hard - log_total)).astype(BF16).astype(F32)
+        term3_ref[:, at] = dot(coef3, q_ref[:, at], ((1,), (0,))).astype(BF16)
+    hard_out[...] = jnp.zeros(hard_out.shape, F32)
+    hard_out[:3] = (w * jnp.exp(hard - log_total)).astype(BF16).astype(F32)
     eye = lax.broadcasted_iota(jnp.int32, (rows, rows), 0) == lax.broadcasted_iota(
         jnp.int32, (rows, rows), 1
     )
     loss_ref[...] = log_total - jnp.sum(jnp.where(eye, scores[0], 0.0), axis=0, keepdims=True)
 
 
-def add_body(a_ref, b_ref, out, token):
+def sums_body(q_ref, other_ref, coef_ref, swap_ref, sent3, partial1, token):
     signal(token)
-    out[...] = (a_ref[...].astype(F32) + b_ref[...].astype(F32)).astype(BF16)
-
-
-def term1_body(q_ref, coef_ref, got2_ref, token, out):
     rows, width = q_ref.shape
-    keep = jnp.where(lax.axis_index("blk") % 2 == 1, 1.0, 0.0)
+    odd = lax.axis_index("blk") % 2 == 1
+    mine = jnp.where(odd, coef_ref[:, rows : 2 * rows], coef_ref[:, 3 * rows :])
+    coef = jnp.concatenate([mine, swap_ref[:, rows:]], axis=1)
     for c in range(0, width, CHUNK):
         at = slice(c, c + CHUNK)
-        term1 = dot(coef_ref[rows : 2 * rows], q_ref[:, at], ((1,), (0,)))
-        out[:, at] = term1 + keep * got2_ref[:, at].astype(F32)
+        held = jnp.concatenate([q_ref[:, at], other_ref[:, at]], axis=0)
+        total = dot(coef, held, ((1,), (0,)))
+        sent3[:, at] = total.astype(BF16)
+        partial1[:, at] = total
 
 
 def relay_body(partial1, got3_ref, out, done):
@@ -202,18 +227,24 @@
 
 
 def base_body(
-    q_ref, p_ref, n1_ref, n2_ref, e3_ref, o3_ref, coef_ref, w_ref, own3_ref, token, pulled, base
+    q_ref, other_ref, p_ref, n1_ref, n2_ref, e3_ref, o3_ref, coef_ref, swap_ref, w_ref, own3_ref,
+    token, pulled, base, coef_t,
 ):
     rows, width = q_ref.shape
     w = jnp.broadcast_to(w_ref[...], (rows, rows)).T[:, :1]
+    odd = lax.axis_index("blk") % 2 == 1
     blocks = (p_ref, n1_ref, n2_ref, e3_ref, o3_ref)
-    coef_t = coef_ref[...].astype(F32).T.astype(BF16)
-    coef_t = jnp.concatenate([coef_t, coef_t[:, 3 * rows :]], axis=1)
+    for s in range(5):
+        k = min(s, 3) * rows
+        coef_t[:, s * rows : (s + 1) * rows] = coef_ref[:, k : k + rows].astype(F32).T.astype(BF16)
+    coef = [coef_ref[:, :rows], jnp.where(odd, swap_ref[:, :rows], jnp.zeros((rows, rows), BF16))]
+    coef = jnp.concatenate(coef, axis=1)
     for c in range(0, width, CHUNK):
         at = slice(c, c + CHUNK)
         held = jnp.concatenate([block[:, at] for block in blocks], axis=0)
-        pulled[:, at] = dot(coef_t, held, ((1,), (0,))) - w * p_ref[:, at].astype(F32)
-        own = dot(coef_ref[:rows], q_ref[:, at], ((1,), (0,))) + own3_ref[:, at].astype(F32)
+        pulled[:, at] = dot(coef_t[...], held, ((1,), (0,))) - w * p_ref[:, at].astype(F32)
+        held = jnp.concatenate([q_ref[:, at], other_ref[:, at]], axis=0)
+        own = dot(coef, held, ((1,), (0,))) + own3_ref[:, at].astype(F32)
         base[:, at] = own - w * q_ref[:, at].astype(F32)
 
 
@@ -249,10 +280,13 @@
     def swap(array):
         return lax.ppermute(array, "blk", [(i, i ^ 1) for i in range(loop)])
 
+    def over_groups(array, r):
+        return lax.ppermute(array, "grp", [(i, i ^ r) for i in range(groups)])
+
     def exchange(arrays):
         out = list(arrays)
         for r in reversed(range(1, groups)):
-            out[r] = lax.ppermute(arrays[r], "grp", [(i, i ^ r) for i in range(groups)])
+            out[r] = over_groups(arrays[r], r)
         return out
 
     def like(*shape, dtype=BF16):
@@ -279,40 +313,51 @@
     next2 = swap(local_call(choose_body, [block], next1, next3_even, flops=LONG)[0])
 
     s0, s1, s3 = local_call(scores_body, [square] * 3, held_q, held_p, next1, next3_even)
-    hard_parts = exchange(
-        local_call(
-            functools.partial(hard_scores_body, groups), [triple] * groups, *pieces, s0, flops=LONG
-        )
-    )
+    half = like(SLOT * groups // 2, rows, dtype=F32)
+    keep, give = local_call(
+        functools.partial(hard_scores_body, groups), [half, half], *pieces, s0, flops=LONG
+    )
+    for bit in range(groups.bit_length() - 2):
+        came = over_groups(give, 1 << bit)
+        half = like(keep.shape[0] // 2, rows, dtype=F32)
+        keep, give = local_call(halve_body, [half, half], keep, came)
+    came = over_groups(give, groups // 2)
+    other_q = swap(held_q)
     (s2,) = local_call(scores_body, [square], held_q, next2)
-    loss_rows, coef, hard_coef, term3, term2 = local_call(
-        functools.partial(weigh_body, groups),
-        [like(1, rows, dtype=F32), like(4 * rows, rows), triple, block, block],
-        held_q, s0, s1, s2, s3, next3_odd, weights[None, :], *hard_parts,
+    loss_rows, coef, hard_coef, to_core, term3 = local_call(
+        weigh_body,
+        [
+            like(1, rows, dtype=F32), like(rows, 4 * rows), like(SLOT, rows, dtype=F32),
+            like(rows, 2 * rows), block,
+        ],
+        held_q, s0, s1, s2, s3, next3_odd, weights[None, :], keep, came, other_q,
     )
 
     got3 = shift(term3, 2, (1,))
-    got2 = swap(term2)
-
-    sent3, token = local_call(add_body, [block, TOKEN], term3, got2)
+    from_core = swap(to_core)
+    sent3, partial1, token = local_call(
+        sums_body, [block, block32, TOKEN], held_q, other_q, coef, from_core
+    )
     own3 = shift(sent3, 3, (0,))
 
-    hard_coefs = exchange([hard_coef] * groups)
+    for bit in range(groups.bit_length() - 1):
+        came = over_groups(hard_coef, 1 << bit)
+        double = like(2 * hard_coef.shape[0], rows, dtype=F32)
+        (hard_coef,) = local_call(double_body, [double], hard_coef, came)
     square_all = pltpu.VMEM((groups * rows, groups * rows), BF16)
     *backs, token = local_call(
         functools.partial(hard_grads_body, groups), [back] * groups + [TOKEN],
-        *pieces, *hard_coefs, token, scratch=[square_all, square_all],
+        *pieces, hard_coef, token, scratch=[square_all, square_all],
     )
     backs = exchange(backs)
 
-    (partial1,) = local_call(term1_body, [block32], held_q, coef, got2, token)
     sent1, token = local_call(relay_body, [block, TOKEN], partial1, got3, flops=SOME)
-    own1 = shift(sent1, 1)
+    own1 = shift(sent1, 1, (1,))
 
     pulled, base = local_call(
         base_body, [block32, block32],
-        held_q, held_p, next1, next2, next3_even, next3_odd, coef, weights[None, :], own3, token,
-        flops=LONG,
+        held_q, other_q, held_p, next1, next2, next3_even, next3_odd, coef, from_core,
+        weights[None, :], own3, token, flops=LONG, scratch=[pltpu.VMEM((rows, 5 * rows), BF16)],
     )
     grad_queries, grad_passages = local_call(
         functools.partial(finish_body, groups), [block, block], pulled, base, own1, *backs,

time: 87.3 us -> 91.6 us (1.049)
  Pallas kernels: 9.96 us -> 18.3 us
  starting transfers between devices: 27.4 us -> 24.4 us
  waiting for transfers between devices: 45.7 us -> 44.5 us
    ppermute x6, waiting for transfers between devices: 36.5 us -> 24 us  [shift(): return lax.ppermute(array, 'blk', pairs)]
    ppermute x12 -> x10, waiting for transfers between devices: 9.13 us -> 20.5 us  [over_groups(): return lax.ppermute(array, 'grp', [(i, i ^ r) for i in range(groups)])]
    pallas_call x13 -> x15, Pallas kernels: 9.96 us -> 18.3 us  [local_call(): pl.pallas_call(body, out_shape=out_shape, in_specs=in_specs or [VMEM] * l...]
    ppermute x12 -> x10, starting transfers between devices: 14.2 us -> 11.7 us  [over_groups(): return lax.ppermute(array, 'grp', [(i, i ^ r) for i in range(groups)])]
    ppermute x6, starting transfers between devices: 12.3 us -> 9.91 us  [shift(): return lax.ppermute(array, 'blk', pairs)]
    ppermute x2 -> x3, starting transfers between devices: 0.84 us -> 2.72 us  [swap(): return lax.ppermute(array, 'blk', [(i, i ^ 1) for i in range(loop)])]
  transfers between devices with their start and end apart: 20 -> 19, of which waited for: 10 -> 11; matrix products, arithmetic and copies ran while one was open for 0% -> 0% of each run, Pallas kernels for 8% -> 16%
where the time goes in v2:
time: 91.6 us; the launch traced here: 91.1 us
  waiting for transfers between devices  44.5 us (49%)
  starting transfers between devices  24.4 us (27%)
  Pallas kernels  18.3 us (20%)
  local copies, waits for them, and re-layouts  3.14 us (3%)
    ppermute x6, waiting for transfers between devices, shift(): return lax.ppermute(array, 'blk', pairs)  24 us
    ppermute x10, waiting for transfers between devices, over_groups(): return lax.ppermute(array, 'grp', [(i, i ^ r) for i in range(groups)])  20.5 us
    pallas_call x15, Pallas kernels, local_call(): pl.pallas_call(body, out_shape=out_shape, in_specs=in_specs or [VMEM] * l...  18.3 us
    ppermute x10, starting transfers between devices, over_groups(): return lax.ppermute(array, 'grp', [(i, i ^ r) for i in range(groups)])  11.7 us
    ppermute x6, starting transfers between devices, shift(): return lax.ppermute(array, 'blk', pairs)  9.91 us
    unnamed x8, local copies, waits for them, and re-layouts  3.14 us
    ppermute x3, starting transfers between devices, swap(): return lax.ppermute(array, 'blk', [(i, i ^ 1) for i in range(loop)])  2.72 us
  transfers between devices with their start and end apart: 19, of which 11 were waited for; matrix products, arithmetic and copies ran while one was open for 0% of the time, Pallas kernels for 16%

profile of v2, /device:TPU:0, one launch (start us, length us, event | category | flops | bytes accessed | tf_op | source)
XLA Modules:
  0.0 91.1 jit_solution(1750588636075786314)
XLA Ops:
  0.6 4.5 %collective-permute-start = (bf16[128,4096]{1,0:T(8,128)(2,1)}, bf16[128,4096]{1,0:T(8,128)(2,1)S(1)}, u32[]{:S(2)}, u32[]{:S(2)}) collective-permute-start(bf16[128,4096]{1,0:T(8,128)(2,1)} %p_hbm.1), channel_id=1, source_target_pairs={{0,7},{1,0},{2,1},{3,2},{4,3},{5,4},{6,5},{7,6},{8,15},{9,8},{10,9... | collective-permute-start | bytes 3145736 | tf_op jit(solution)/shard_map/ppermute | solution.py:278
  5.2 1.2 %copy-done = bf16[128,4096]{1,0:T(8,128)(2,1)S(1)} copy-done((bf16[128,4096]{1,0:T(8,128)(2,1)S(1)}, bf16[128,4096]{1,0:T(8,128)(2,1)}, u32[]{:S(2)}) %copy-start) | copy-done | bytes 1048600
  6.4 1.2 %copy-done.1 = bf16[128,4096]{1,0:T(8,128)(2,1)S(1)} copy-done((bf16[128,4096]{1,0:T(8,128)(2,1)S(1)}, bf16[128,4096]{1,0:T(8,128)(2,1)}, u32[]{:S(2)}) %copy-start.1) | copy-done | bytes 1048600
  8.3 1.3 %shard_map.67 = (bf16[128,4096]{1,0:T(8,128)(2,1)}, bf16[128,4096]{1,0:T(8,128)(2,1)S(1)}, bf16[272,1024]{1,0:T(8,128)(2,1)S(1)}, bf16[272,1024]{1,0:T(8,128)(2,...) custom-call(bf16[128,4096]{1,0:T(8,128)(2,1)S(1)} %copy-done, ...), custom_call_target="tpu_custom_call" | custom-call | bytes 6428160 | tf_op jit(solution)/shard_map/pallas_call | solution.py:32
  9.6 1.3 %collective-permute-start.1 = (bf16[128,4096]{1,0:T(8,128)(2,1)S(1)}, bf16[128,4096]{1,0:T(8,128)(2,1)S(1)}, u32[]{:S(2)}, u32[]{:S(2)}) collective-permute-start(bf16[128,4096]{1,0:T(8,128)(2,1)S(1)} %get-tuple-element.36.refs_0_.p_ref), channel_id=1, source_target_pairs={{1,6},{3,0},{5,2},{7,4},{9,14},{11,8},{13,10},{15,12},{17,22},{19,... | collective-permute-start | bytes 3145736 | tf_op jit(solution)/shard_map/ppermute | solution.py:278
  10.9 1.6 %collective-permute-start.4 = (bf16[272,1024]{1,0:T(8,128)(2,1)S(1)}, bf16[272,1024]{1,0:T(8,128)(2,1)S(1)}, u32[]{:S(2)}, u32[]{:S(2)}) collective-permute-start(bf16[272,1024]{1,0:T(8,128)(2,1)S(1)} %get-tuple-element.42), channel_id=1, source_target_pairs={{0,8},{8,0},{16,24},{24,16},{1,9},{9,1},{17,25},{25,17},{2,10},{10... | collective-permute-start | bytes 1671176 | tf_op jit(solution)/shard_map/ppermute | solution.py:284
  12.5 1.5 %collective-permute-start.5 = (bf16[272,1024]{1,0:T(8,128)(2,1)S(1)}, bf16[272,1024]{1,0:T(8,128)(2,1)S(1)}, u32[]{:S(2)}, u32[]{:S(2)}) collective-permute-start(bf16[272,1024]{1,0:T(8,128)(2,1)S(1)} %get-tuple-element.43), channel_id=1, source_target_pairs={{0,16},{8,24},{16,0},{24,8},{1,17},{9,25},{17,1},{25,9},{2,18},{10... | collective-permute-start | bytes 1671176 | tf_op jit(solution)/shard_map/ppermute | solution.py:284
  14.5 8.4 %collective-permute-done.source = bf16[128,4096]{1,0:T(8,128)(2,1)S(1)} collective-permute-done((bf16[128,4096]{1,0:T(8,128)(2,1)}, bf16[128,4096]{1,0:T(8,128)(2,1)S(1)}, u32[]{:S(2)}, u32[]{:S(2)}) %collective-permute-start) | collective-permute-done | bytes 1048608 | tf_op jit(solution)/shard_map/ppermute | solution.py:278
  22.9 5.0 %collective-permute-done.1.refs_2_.e3_ref = bf16[128,4096]{1,0:T(8,128)(2,1)S(1)} collective-permute-done((bf16[128,4096]{1,0:T(8,128)(2,1)S(1)}, bf16[128,4096]{1,0:T(8,128)(2,1)S(1)}, u32[]{:S(2)}, u32[]{:S(2)}) %collective-permute-start.1) | collective-permute-done | bytes 1048608 | tf_op jit(solution)/shard_map/ppermute | solution.py:278
  28.7 2.2 %shard_map.69 = (f32[128,128]{1,0:T(8,128)S(1)}, f32[128,128]{1,0:T(8,128)S(1)}, f32[128,128]{1,0:T(8,128)S(1)}) custom-call(bf16[128,4096]{1,0:T(8,128)(2,1)} %get-tuple-element.35.q_ref, bf16[128,4096]{1,0:T(8,128)(2,1)S(1)} %get-tuple-element.36.refs_0_.p_ref, bf16[128,4096]{1,0:T(8,128)(2,1)S(1)} %shard_map.68.refs_1_.n1_ref, ...), custom_call_target="tpu_custom_call" | custom-call | bytes 4390912 | tf_op jit(solution)/shard_map/pallas_call | solution.py:32
  31.0 2.7 %collective-permute-start.2 = (bf16[128,4096]{1,0:T(8,128)(2,1)S(1)}, bf16[128,4096]{1,0:T(8,128)(2,1)S(1)}, u32[]{:S(2)}, u32[]{:S(2)}) collective-permute-start(bf16[128,4096]{1,0:T(8,128)(2,1)S(1)} %shard_map.70), channel_id=1, source_target_pairs={{0,1},{1,0},{2,3},{3,2},{4,5},{5,4},{6,7},{7,6},{8,9},{9,8},{10,11... | collective-permute-start | bytes 3145736 | tf_op jit(solution)/shard_map/ppermute | solution.py:281
  33.6 6.2 %collective-permute-done.5.refs_2_ = bf16[272,1024]{1,0:T(8,128)(2,1)S(1)} collective-permute-done((bf16[272,1024]{1,0:T(8,128)(2,1)S(1)}, bf16[272,1024]{1,0:T(8,128)(2,1)S(1)}, u32[]{:S(2)}, u32[]{:S(2)}) %collective-permute-start.5) | collective-permute-done | bytes 557088 | tf_op jit(solution)/shard_map/ppermute | solution.py:284
  39.8 1.4 %shard_map.72 = (f32[16,128]{1,0:T(8,128)S(1)}, f32[16,128]{1,0:T(8,128)S(1)}) custom-call(bf16[272,1024]{1,0:T(8,128)(2,1)S(1)} %get-tuple-element.41.refs_0_, bf16[272,1024]{1,0:T(8,128)(2,1)S(1)} %collective-permute-done.4.refs_1_, bf16[272,1024]{1,0:T(8,128)(2,1)S(1)} %collective-permute-done.5.refs_2_, ...), custom_call_target="tpu_custom_call" | custom-call | flops 49999998976 | bytes 2310144 | tf_op jit(solution)/shard_map/pallas_call | solution.py:32
  42.1 2.9 %collective-permute-done.7.came_ref = f32[16,128]{1,0:T(8,128)S(1)} collective-permute-done((f32[16,128]{1,0:T(8,128)S(1)}, f32[16,128]{1,0:T(8,128)S(1)}, u32[]{:S(2)}, u32[]{:S(2)}) %collective-permute-start.7) | collective-permute-done | bytes 8224 | tf_op jit(solution)/shard_map/ppermute | solution.py:284
  45.0 1.5 %collective-permute-start.8 = (f32[8,128]{1,0:T(8,128)S(1)}, f32[8,128]{1,0:T(8,128)S(1)}, u32[]{:S(2)}, u32[]{:S(2)}) collective-permute-start(f32[8,128]{1,0:T(8,128)S(1)} %get-tuple-element.48), channel_id=1, source_target_pairs={{0,16},{8,24},{16,0},{24,8},{1,17},{9,25},{17,1},{25,9},{2,18},{10... | collective-permute-start | bytes 12296 | tf_op jit(solution)/shard_map/ppermute | solution.py:284
  46.5 1.7 %shard_map.71.s2_ref = f32[128,128]{1,0:T(8,128)S(1)} custom-call(bf16[128,4096]{1,0:T(8,128)(2,1)} %get-tuple-element.35.q_ref, bf16[128,4096]{1,0:T(8,128)(2,1)S(1)} %collective-permute-done.2.refs_0_.n2_ref), custom_call_target="tpu_custom_call" | custom-call | bytes 2162688 | tf_op jit(solution)/shard_map/pallas_call | solution.py:32
  48.6 2.6 %shard_map.74 = (f32[1,128]{1,0:T(1,128)}, bf16[128,512]{1,0:T(8,128)(2,1)S(1)}, f32[8,128]{1,0:T(8,128)S(1)}, bf16[128,256]{1,0:T(8,128)(2,1)S(1)}, bf16[128,4096]{1,0:T(8,128)(2,1)S(1)}) custom-call(bf16[128,4096]{1,0:T(8,128)(2,1)} %get-tuple-element.35.q_ref, f32[128,128]{1,0:T(8,128)S(1)} %get-tuple-element.38.refs_4_.s0_ref, ...), custom_call_target="tpu_custom_call" | custom-call | bytes 4666368 | tf_op jit(solution)/shard_map/pallas_call | solution.py:32
  52.0 0.8 collective-permute-start.14
  52.9 2.8 %collective-permute-done.14.came_ref = f32[8,128]{1,0:T(8,128)S(1)} collective-permute-done((f32[8,128]{1,0:T(8,128)S(1)}, f32[8,128]{1,0:T(8,128)S(1)}, u32[]{:S(2)}, u32[]{:S(2)}) %collective-permute-start.14) | collective-permute-done | bytes 4128 | tf_op jit(solution)/shard_map/ppermute | solution.py:284
  55.7 1.5 %collective-permute-start.15 = (f32[16,128]{1,0:T(8,128)S(1)}, f32[16,128]{1,0:T(8,128)S(1)}, u32[]{:S(2)}, u32[]{:S(2)}) collective-permute-start(f32[16,128]{1,0:T(8,128)S(1)} %shard_map.78.mine_ref), channel_id=1, source_target_pairs={{0,16},{8,24},{16,0},{24,8},{1,17},{9,25},{17,1},{25,9},{2,18},{10... | collective-permute-start | bytes 24584 | tf_op jit(solution)/shard_map/ppermute | solution.py:284
  57.2 2.1 %collective-permute-done.15.came_ref = f32[16,128]{1,0:T(8,128)S(1)} collective-permute-done((f32[16,128]{1,0:T(8,128)S(1)}, f32[16,128]{1,0:T(8,128)S(1)}, u32[]{:S(2)}, u32[]{:S(2)}) %collective-permute-start.15) | collective-permute-done | bytes 8224 | tf_op jit(solution)/shard_map/ppermute | solution.py:284
  59.4 2.0 %shard_map.75 = (bf16[128,4096]{1,0:T(8,128)(2,1)S(1)}, f32[128,4096]{1,0:T(8,128)S(1)}, f32[8,128]{1,0:T(8,128)S(1)}) custom-call(bf16[128,4096]{1,0:T(8,128)(2,1)} %get-tuple-element.35.q_ref, bf16[128,4096]{1,0:T(8,128)(2,1)} %collective-permute-done.9.other_ref, bf16[128,512]{1,0:T(8,128)(2,1)S(1)} %get-tuple-element.50.coef_ref, ...), custom_call_target="tpu_custom_call" | custom-call | bytes 5443584 | tf_op jit(solution)/shard_map/pallas_call | solution.py:32
  61.4 1.4 %collective-permute-start.11 = (bf16[128,4096]{1,0:T(8,128)(2,1)S(1)}, bf16[128,4096]{1,0:T(8,128)(2,1)S(1)}, u32[]{:S(2)}, u32[]{:S(2)}) collective-permute-start(bf16[128,4096]{1,0:T(8,128)(2,1)S(1)} %get-tuple-element.52), channel_id=1, source_target_pairs={{0,3},{2,5},{4,7},{6,1},{8,11},{10,13},{12,15},{14,9},{16,19},{18,... | collective-permute-start | bytes 3145736 | tf_op jit(solution)/shard_map/ppermute | solution.py:278
  62.7 2.1 %shard_map.80 = (bf16[256,1024]{1,0:T(8,128)(2,1)S(1)}, bf16[256,1024]{1,0:T(8,128)(2,1)S(1)}, bf16[256,1024]{1,0:T(8,128)(2,1)S(1)}, bf16[256,1024]{1,0:T(8,128)(2,1)S(1)}, f32[8,128]{1,0:T(8,128)}) custom-call(bf16[272,1024]{1,0:T(8,128)(2,1)S(1)} %get-tuple-element.41.refs_0_, bf16[272,1024]{1,0:T(8,128)(2,1)S(1)} %collective-permute-done.4.refs_1_, ...), custom_call_target="tpu_custom_call" | custom-call | bytes 4349952 | tf_op jit(solution)/shard_map/pallas_call | solution.py:32
  65.6 1.3 %collective-permute-start.17 = (bf16[256,1024]{1,0:T(8,128)(2,1)S(1)}, bf16[256,1024]{1,0:T(8,128)(2,1)S(1)}, u32[]{:S(2)}, u32[]{:S(2)}) collective-permute-start(bf16[256,1024]{1,0:T(8,128)(2,1)S(1)} %get-tuple-element.63), channel_id=1, source_target_pairs={{0,16},{8,24},{16,0},{24,8},{1,17},{9,25},{17,1},{25,9},{2,18},{10... | collective-permute-start | bytes 1572872 | tf_op jit(solution)/shard_map/ppermute | solution.py:284
  66.9 1.4 %collective-permute-start.18 = (bf16[256,1024]{1,0:T(8,128)(2,1)S(1)}, bf16[256,1024]{1,0:T(8,128)(2,1)S(1)}, u32[]{:S(2)}, u32[]{:S(2)}) collective-permute-start(bf16[256,1024]{1,0:T(8,128)(2,1)S(1)} %get-tuple-element.64), channel_id=1, source_target_pairs={{0,24},{8,16},{16,8},{24,0},{1,25},{9,17},{17,9},{25,1},{2,26},{10... | collective-permute-start | bytes 1572872 | tf_op jit(solution)/shard_map/ppermute | solution.py:284
  68.5 1.3 %collective-permute-start.13 = (bf16[128,4096]{1,0:T(8,128)(2,1)S(1)}, bf16[128,4096]{1,0:T(8,128)(2,1)S(1)}, u32[]{:S(2)}, u32[]{:S(2)}) collective-permute-start(bf16[128,4096]{1,0:T(8,128)(2,1)S(1)} %get-tuple-element.58), channel_id=1, source_target_pairs={{1,2},{3,4},{5,6},{7,0},{9,10},{11,12},{13,14},{15,8},{17,18},{19,... | collective-permute-start | bytes 3145736 | tf_op jit(solution)/shard_map/ppermute | solution.py:278
  69.8 9.9 %collective-permute-done.11.own3_ref = bf16[128,4096]{1,0:T(8,128)(2,1)S(1)} collective-permute-done((bf16[128,4096]{1,0:T(8,128)(2,1)S(1)}, bf16[128,4096]{1,0:T(8,128)(2,1)S(1)}, u32[]{:S(2)}, u32[]{:S(2)}) %collective-permute-start.11) | collective-permute-done | bytes 1048608 | tf_op jit(solution)/shard_map/ppermute | solution.py:278
  79.6 3.2 %shard_map.77 = (f32[128,4096]{1,0:T(8,128)S(1)}, f32[128,4096]{1,0:T(8,128)S(1)}) custom-call(bf16[128,4096]{1,0:T(8,128)(2,1)} %get-tuple-element.35.q_ref, bf16[128,4096]{1,0:T(8,128)(2,1)} %collective-permute-done.9.other_ref, bf16[128,4096]{1,0:T(8,128)(2,1)S(1)} %get-tuple-element.36.refs_0_.p_ref, bf16[128,4096]{1,0:T(8,128)(2,1)S(1)} %shard_map.68.refs_1_.n1_ref, ...), custom_call_target="tpu_custom_call" | custom-call | flops 49999998976 | bytes 12784128 | tf_op jit(solution)/shard_map/pallas_call | solution.py:32
  82.8 4.5 %collective-permute-done.17.refs_2_ = bf16[256,1024]{1,0:T(8,128)(2,1)S(1)} collective-permute-done((bf16[256,1024]{1,0:T(8,128)(2,1)S(1)}, bf16[256,1024]{1,0:T(8,128)(2,1)S(1)}, u32[]{:S(2)}, u32[]{:S(2)}) %collective-permute-start.17) | collective-permute-done | bytes 524320 | tf_op jit(solution)/shard_map/ppermute | solution.py:284
  87.3 1.6 %collective-permute-done.18.refs_3_ = bf16[256,1024]{1,0:T(8,128)(2,1)S(1)} collective-permute-done((bf16[256,1024]{1,0:T(8,128)(2,1)S(1)}, bf16[256,1024]{1,0:T(8,128)(2,1)S(1)}, u32[]{:S(2)}, u32[]{:S(2)}) %collective-permute-start.18) | collective-permute-done | bytes 524320 | tf_op jit(solution)/shard_map/ppermute | solution.py:284
  89.6 1.5 %shard_map.81 = (bf16[128,4096]{1,0:T(8,128)(2,1)}, bf16[128,4096]{1,0:T(8,128)(2,1)}) custom-call(f32[128,4096]{1,0:T(8,128)S(1)} %get-tuple-element.56.pulled, f32[128,4096]{1,0:T(8,128)S(1)} %get-tuple-element.57.base, bf16[128,4096]{1,0:T(8,128)(2,1)S(1)} %collective-permute-done.13.own1, bf16[256,1024]{1,0:T(8,128)(2,1)S(1)} %get-tuple-element.61.refs_0_, ...), custom_call_target="tpu_custom_call" | custom-call | bytes 9437184 | tf_op jit(solution)/shard_map/pallas_call | solution.py:32
  (29 shorter events, 5.8 us)
Async XLA Ops:
  0.6 22.2 %collective-permute-start = (bf16[128,4096]{1,0:T(8,128)(2,1)}, bf16[128,4096]{1,0:T(8,128)(2,1)S(1)}, u32[]{:S(2)}, u32[]{:S(2)}) collective-permute-start(bf16[128,4096]{1,0:T(8,128)(2,1)} %p_hbm.1), channel_id=1, source_target_pairs={{0,7},{1,0},{2,1},{3,2},{4,3},{5,4},{6,5},{7,6},{8,15},{9,8},{10,9... | collective-permute-start | bytes 3145736 | tf_op jit(solution)/shard_map/ppermute | solution.py:278
  5.2 1.2 %copy-start = (bf16[128,4096]{1,0:T(8,128)(2,1)S(1)}, bf16[128,4096]{1,0:T(8,128)(2,1)}, u32[]{:S(2)}) copy-start(bf16[128,4096]{1,0:T(8,128)(2,1)} %q_hbm.1) | copy-start | bytes 3145732
  6.4 1.2 %copy-start.1 = (bf16[128,4096]{1,0:T(8,128)(2,1)S(1)}, bf16[128,4096]{1,0:T(8,128)(2,1)}, u32[]{:S(2)}) copy-start(bf16[128,4096]{1,0:T(8,128)(2,1)} %p_hbm.1) | copy-start | bytes 3145732
  7.6 0.7 copy-start.2
  9.6 18.3 %collective-permute-start.1 = (bf16[128,4096]{1,0:T(8,128)(2,1)S(1)}, bf16[128,4096]{1,0:T(8,128)(2,1)S(1)}, u32[]{:S(2)}, u32[]{:S(2)}) collective-permute-start(bf16[128,4096]{1,0:T(8,128)(2,1)S(1)} %get-tuple-element.36.refs_0_.p_ref), channel_id=1, source_target_pairs={{1,6},{3,0},{5,2},{7,4},{9,14},{11,8},{13,10},{15,12},{17,22},{19,... | collective-permute-start | bytes 3145736 | tf_op jit(solution)/shard_map/ppermute | solution.py:278
  10.9 20.0 %collective-permute-start.4 = (bf16[272,1024]{1,0:T(8,128)(2,1)S(1)}, bf16[272,1024]{1,0:T(8,128)(2,1)S(1)}, u32[]{:S(2)}, u32[]{:S(2)}) collective-permute-start(bf16[272,1024]{1,0:T(8,128)(2,1)S(1)} %get-tuple-element.42), channel_id=1, source_target_pairs={{0,8},{8,0},{16,24},{24,16},{1,9},{9,1},{17,25},{25,17},{2,10},{10... | collective-permute-start | bytes 1671176 | tf_op jit(solution)/shard_map/ppermute | solution.py:284
  12.5 27.3 %collective-permute-start.5 = (bf16[272,1024]{1,0:T(8,128)(2,1)S(1)}, bf16[272,1024]{1,0:T(8,128)(2,1)S(1)}, u32[]{:S(2)}, u32[]{:S(2)}) collective-permute-start(bf16[272,1024]{1,0:T(8,128)(2,1)S(1)} %get-tuple-element.43), channel_id=1, source_target_pairs={{0,16},{8,24},{16,0},{24,8},{1,17},{9,25},{17,1},{25,9},{2,18},{10... | collective-permute-start | bytes 1671176 | tf_op jit(solution)/shard_map/ppermute | solution.py:284
  14.0 25.8 %collective-permute-start.6 = (bf16[272,1024]{1,0:T(8,128)(2,1)S(1)}, bf16[272,1024]{1,0:T(8,128)(2,1)S(1)}, u32[]{:S(2)}, u32[]{:S(2)}) collective-permute-start(bf16[272,1024]{1,0:T(8,128)(2,1)S(1)} %get-tuple-element.44), channel_id=1, source_target_pairs={{0,24},{8,16},{16,8},{24,0},{1,25},{9,17},{17,9},{25,1},{2,26},{10... | collective-permute-start | bytes 1671176 | tf_op jit(solution)/shard_map/ppermute | solution.py:284
  22.8 25.3 %collective-permute-start.9 = (bf16[128,4096]{1,0:T(8,128)(2,1)}, bf16[128,4096]{1,0:T(8,128)(2,1)}, u32[]{:S(2)}, u32[]{:S(2)}) collective-permute-start(bf16[128,4096]{1,0:T(8,128)(2,1)} %get-tuple-element.35.q_ref), channel_id=1, source_target_pairs={{0,1},{1,0},{2,3},{3,2},{4,5},{5,4},{6,7},{7,6},{8,9},{9,8},{10,11... | collective-permute-start | bytes 3145736 | tf_op jit(solution)/shard_map/ppermute | solution.py:281
  27.9 20.6 %collective-permute-start.3 = (bf16[128,4096]{1,0:T(8,128)(2,1)S(1)}, bf16[128,4096]{1,0:T(8,128)(2,1)S(1)}, u32[]{:S(2)}, u32[]{:S(2)}) collective-permute-start(bf16[128,4096]{1,0:T(8,128)(2,1)S(1)} %shard_map.68.refs_1_.n1_ref), channel_id=1, source_target_pairs={{1,7},{3,1},{5,3},{7,5},{9,15},{11,9},{13,11},{15,13},{17,23},{19,... | collective-permute-start | bytes 3145736 | tf_op jit(solution)/shard_map/ppermute | solution.py:278
  31.0 15.5 %collective-permute-start.2 = (bf16[128,4096]{1,0:T(8,128)(2,1)S(1)}, bf16[128,4096]{1,0:T(8,128)(2,1)S(1)}, u32[]{:S(2)}, u32[]{:S(2)}) collective-permute-start(bf16[128,4096]{1,0:T(8,128)(2,1)S(1)} %shard_map.70), channel_id=1, source_target_pairs={{0,1},{1,0},{2,3},{3,2},{4,5},{5,4},{6,7},{7,6},{8,9},{9,8},{10,11... | collective-permute-start | bytes 3145736 | tf_op jit(solution)/shard_map/ppermute | solution.py:281
  41.2 7.3 %copy-start.3 = (f32[128]{0:T(128)S(1)}, f32[128]{0:T(128)}, u32[]{:S(2)}) copy-start(f32[128]{0:T(128)} %param.7) | copy-start | bytes 1540
  41.2 3.7 %collective-permute-start.7 = (f32[16,128]{1,0:T(8,128)S(1)}, f32[16,128]{1,0:T(8,128)S(1)}, u32[]{:S(2)}, u32[]{:S(2)}) collective-permute-start(f32[16,128]{1,0:T(8,128)S(1)} %get-tuple-element.46), channel_id=1, source_target_pairs={{0,8},{8,0},{16,24},{24,16},{1,9},{9,1},{17,25},{25,17},{2,10},{10... | collective-permute-start | bytes 24584 | tf_op jit(solution)/shard_map/ppermute | solution.py:284
  45.0 3.6 %collective-permute-start.8 = (f32[8,128]{1,0:T(8,128)S(1)}, f32[8,128]{1,0:T(8,128)S(1)}, u32[]{:S(2)}, u32[]{:S(2)}) collective-permute-start(f32[8,128]{1,0:T(8,128)S(1)} %get-tuple-element.48), channel_id=1, source_target_pairs={{0,16},{8,24},{16,0},{24,8},{1,17},{9,25},{17,1},{25,9},{2,18},{10... | collective-permute-start | bytes 12296 | tf_op jit(solution)/shard_map/ppermute | solution.py:284
  51.2 17.1 %collective-permute-start.12 = (bf16[128,4096]{1,0:T(8,128)(2,1)S(1)}, bf16[128,4096]{1,0:T(8,128)(2,1)S(1)}, u32[]{:S(2)}, u32[]{:S(2)}) collective-permute-start(bf16[128,4096]{1,0:T(8,128)(2,1)S(1)} %get-tuple-element.54), channel_id=1, source_target_pairs={{1,3},{3,5},{5,7},{7,1},{9,11},{11,13},{13,15},{15,9},{17,19},{19,... | collective-permute-start | bytes 3145736 | tf_op jit(solution)/shard_map/ppermute | solution.py:278
  52.0 7.4 %collective-permute-start.10 = (bf16[128,256]{1,0:T(8,128)(2,1)S(1)}, bf16[128,256]{1,0:T(8,128)(2,1)S(1)}, u32[]{:S(2)}, u32[]{:S(2)}) collective-permute-start(bf16[128,256]{1,0:T(8,128)(2,1)S(1)} %get-tuple-element.51), channel_id=1, source_target_pairs={{0,1},{1,0},{2,3},{3,2},{4,5},{5,4},{6,7},{7,6},{8,9},{9,8},{10,11... | collective-permute-start | bytes 196616 | tf_op jit(solution)/shard_map/ppermute | solution.py:281
  52.0 3.7 %collective-permute-start.14 = (f32[8,128]{1,0:T(8,128)S(1)}, f32[8,128]{1,0:T(8,128)S(1)}, u32[]{:S(2)}, u32[]{:S(2)}) collective-permute-start(f32[8,128]{1,0:T(8,128)S(1)} %get-tuple-element.59.mine_ref), channel_id=1, source_target_pairs={{0,8},{8,0},{16,24},{24,16},{1,9},{9,1},{17,25},{25,17},{2,10},{10... | collective-permute-start | bytes 12296 | tf_op jit(solution)/shard_map/ppermute | solution.py:284
  55.7 3.7 %collective-permute-start.15 = (f32[16,128]{1,0:T(8,128)S(1)}, f32[16,128]{1,0:T(8,128)S(1)}, u32[]{:S(2)}, u32[]{:S(2)}) collective-permute-start(f32[16,128]{1,0:T(8,128)S(1)} %shard_map.78.mine_ref), channel_id=1, source_target_pairs={{0,16},{8,24},{16,0},{24,8},{1,17},{9,25},{17,1},{25,9},{2,18},{10... | collective-permute-start | bytes 24584 | tf_op jit(solution)/shard_map/ppermute | solution.py:284
  61.4 18.3 %collective-permute-start.11 = (bf16[128,4096]{1,0:T(8,128)(2,1)S(1)}, bf16[128,4096]{1,0:T(8,128)(2,1)S(1)}, u32[]{:S(2)}, u32[]{:S(2)}) collective-permute-start(bf16[128,4096]{1,0:T(8,128)(2,1)S(1)} %get-tuple-element.52), channel_id=1, source_target_pairs={{0,3},{2,5},{4,7},{6,1},{8,11},{10,13},{12,15},{14,9},{16,19},{18,... | collective-permute-start | bytes 3145736 | tf_op jit(solution)/shard_map/ppermute | solution.py:278
  64.8 18.0 %collective-permute-start.16 = (bf16[256,1024]{1,0:T(8,128)(2,1)S(1)}, bf16[256,1024]{1,0:T(8,128)(2,1)S(1)}, u32[]{:S(2)}, u32[]{:S(2)}) collective-permute-start(bf16[256,1024]{1,0:T(8,128)(2,1)S(1)} %get-tuple-element.62), channel_id=1, source_target_pairs={{0,8},{8,0},{16,24},{24,16},{1,9},{9,1},{17,25},{25,17},{2,10},{10... | collective-permute-start | bytes 1572872 | tf_op jit(solution)/shard_map/ppermute | solution.py:284
  65.6 21.7 %collective-permute-start.17 = (bf16[256,1024]{1,0:T(8,128)(2,1)S(1)}, bf16[256,1024]{1,0:T(8,128)(2,1)S(1)}, u32[]{:S(2)}, u32[]{:S(2)}) collective-permute-start(bf16[256,1024]{1,0:T(8,128)(2,1)S(1)} %get-tuple-element.63), channel_id=1, source_target_pairs={{0,16},{8,24},{16,0},{24,8},{1,17},{9,25},{17,1},{25,9},{2,18},{10... | collective-permute-start | bytes 1572872 | tf_op jit(solution)/shard_map/ppermute | solution.py:284
  66.9 22.0 %collective-permute-start.18 = (bf16[256,1024]{1,0:T(8,128)(2,1)S(1)}, bf16[256,1024]{1,0:T(8,128)(2,1)S(1)}, u32[]{:S(2)}, u32[]{:S(2)}) collective-permute-start(bf16[256,1024]{1,0:T(8,128)(2,1)S(1)} %get-tuple-element.64), channel_id=1, source_target_pairs={{0,24},{8,16},{16,8},{24,0},{1,25},{9,17},{17,9},{25,1},{2,26},{10... | collective-permute-start | bytes 1572872 | tf_op jit(solution)/shard_map/ppermute | solution.py:284
  68.5 21.2 %collective-permute-start.13 = (bf16[128,4096]{1,0:T(8,128)(2,1)S(1)}, bf16[128,4096]{1,0:T(8,128)(2,1)S(1)}, u32[]{:S(2)}, u32[]{:S(2)}) collective-permute-start(bf16[128,4096]{1,0:T(8,128)(2,1)S(1)} %get-tuple-element.58), channel_id=1, source_target_pairs={{1,2},{3,4},{5,6},{7,0},{9,10},{11,12},{13,14},{15,8},{17,18},{19,... | collective-permute-start | bytes 3145736 | tf_op jit(solution)/shard_map/ppermute | solution.py:278
